TPU v7x, 32 devices: a whole 2x2x4 slice. The times are simulated.
32 devices in a mesh: branch: 4 (over y, x), seq: 8 (over z, core).
Axes of the slice: x: 2, y: 2, z: 4, core: 2. Of those that a mesh axis runs over, the one named last changes fastest.
Arguments:
- x_in: bfloat16 [4096, 1024], P(('seq', 'branch')), may hold values from -6 to 6
- lengths: int32 [5], replicated, may hold values from 64 to 3712, as said below
- norm1_gain: float32 [1024], replicated, may hold values from 0.5 to 1.5
- w_mix_in: bfloat16 [1024, 3584], P('seq', 'branch'), may hold values from -0.1875 to 0.1875
- w_dt: bfloat16 [1024, 24], P('seq', 'branch'), may hold values from -0.1875 to 0.1875
- w_shared: bfloat16 [1024, 512], P('seq'), may hold values from -0.1875 to 0.1875
- conv_x: float32 [4, 1536], P(None, 'branch'), may hold values from -3 to 3
- conv_bc: float32 [4, 256], replicated, may hold values from -3 to 3
- a_log: float32 [24], P('branch'), may hold values from -3 to 1
- dt_bias: float32 [24], P('branch'), may hold values from -8 to -2
- d_skip: float32 [24], P('branch'), may hold values from 0.5 to 1.5
- gate_gain: float32 [1536], replicated, may hold values from 0.5 to 1.5
- w_out: bfloat16 [2048, 1024], P('seq'), may hold values from -0.1875 to 0.1875
- norm2_gain: float32 [1024], replicated, may hold values from 0.5 to 1.5
- w_gate: bfloat16 [1024, 2048], P('seq'), may hold values from -0.1875 to 0.1875
- w_up: bfloat16 [1024, 2048], P('seq'), may hold values from -0.1875 to 0.1875
- w_down: bfloat16 [2048, 1024], P('seq'), may hold values from -0.125 to 0.125
- d_out: bfloat16 [4096, 1024], P(('seq', 'branch')), may hold values from -6 to 6
Outputs:
- y_out: bfloat16 [4096, 1024], P(('seq', 'branch'))
- grad_x: float32 [4096, 1024], P(('seq', 'branch'))
- grad_norm1_gain: float32 [1024], P(('branch', 'seq'))
- grad_w_mix_in: float32 [1024, 3584], P('seq', 'branch')
- grad_w_dt: float32 [1024, 24], P('seq', 'branch')
- grad_w_shared: float32 [1024, 512], P(('branch', 'seq'))
- grad_conv_x: float32 [4, 1536], P(None, ('branch', 'seq'))
- grad_conv_bc: float32 [4, 256], P(None, ('branch', 'seq'))
- grad_a_log: float32 [24], P('branch')
- grad_dt_bias: float32 [24], P('branch')
- grad_d_skip: float32 [24], P('branch')
- grad_gate_gain: float32 [1536], P(('branch', 'seq'))
- grad_w_out: float32 [2048, 1024], P(('branch', 'seq'))
- grad_norm2_gain: float32 [1024], P(('branch', 'seq'))
- grad_w_gate: float32 [1024, 2048], P(('branch', 'seq'))
- grad_w_up: float32 [1024, 2048], P(('branch', 'seq'))
- grad_w_down: float32 [2048, 1024], P(('branch', 'seq'))
Inputs may be any that keep to these rules, and one draw needn't show every extreme that they name: The 5 lengths sum to 4096. One sequence, at a place among them drawn from the seed, begins within the first 512 rows and ends within the last 512 rows; every other one has from an eighth to a quarter of 512 rows.
All inputs are finite; a program needn't handle non-finite values.
Results may differ from a plain program's by a relative error of at most 0.024.
Values may be sent and summed in bfloat16 or wider, within the bound.
No kernel may reach another device: no remote copies, remote signals or barrier semaphores. Data moves between devices by JAX's collectives and lax.ppermute only.
A program may use at most 448 MiB of HBM per device.

v0:
```python
import jax
import jax.numpy as jnp
from jax import lax
from jax.sharding import PartitionSpec as P

HEADS_ATT = 8
KV = 2
HEAD = 64
CONV = 4
SPAN = 128


HIGHEST = lax.Precision.HIGHEST
EPSILON = 1e-06
SCORE_SCALE = 0.125
ROPE_BASE = 1000000.0


def from_behind(block, axis, distance):
    devices = range(lax.axis_size(axis))
    route = [(i - distance, i) for i in devices if i - distance in devices]
    return lax.ppermute(block, axis, route)


def entering_2(shard, axis, combine, identity):
    count, position = (lax.axis_size(axis), lax.axis_index(axis))
    everything = jax.tree.map(
        lambda part, kind: lax.all_gather(part.astype(kind), axis),
        shard,
        (jnp.bfloat16, jnp.bfloat16),
    )
    start = jax.tree.map(
        lambda part, zero: jnp.broadcast_to(jnp.asarray(zero, part.dtype), part.shape),
        shard,
        identity,
    )

    def turn(k, before):
        reached = k < position
        new = combine(
            before, jax.tree.map(lambda part, own: part[k].astype(own.dtype), everything, shard)
        )
        return jax.tree.map(lambda a, b: jnp.where(reached, a, b), new, before)

    return lax.fori_loop(0, count, turn, start)


def entering_3(shard, axis, combine, identity):
    count, position = (lax.axis_size(axis), lax.axis_index(axis))
    everything = jax.tree.map(
        lambda part, kind: lax.all_gather(part.astype(kind), axis),
        shard,
        jax.tree.map(lambda a: jnp.bfloat16 if a.dtype == jnp.float32 else a.dtype, shard),
    )
    start = jax.tree.map(
        lambda part, zero: jnp.broadcast_to(jnp.asarray(zero, part.dtype), part.shape),
        shard,
        identity,
    )

    def turn(k, before):
        at = count - 1 - k
        reached = at > position
        new = combine(
            before, jax.tree.map(lambda part, own: part[at].astype(own.dtype), everything, shard)
        )
        return jax.tree.map(lambda a, b: jnp.where(reached, a, b), new, before)

    return lax.fori_loop(0, count, turn, start)


def split_up(shard, dim, count):
    before, after = (shard.shape[:dim], shard.shape[dim + 1 :])
    return jnp.moveaxis(shard.reshape(*before, count, -1, *after), dim, 0)


def sent_and_summed(shard, axis, dim):
    count = lax.axis_size(axis)
    blocks = lax.all_to_all(split_up(shard, dim, count), axis, 0, 0, tiled=True)
    return jnp.sum(blocks.astype(jnp.float32), axis=0)


def side_by_side(arrays, axis, dim, along):
    widths = [a.shape[along] for a in arrays]
    both = jnp.concatenate(arrays, axis=along)
    result = sent_and_summed(both, axis, dim)
    return tuple(jnp.split(result, [sum(widths[:k]) for k in range(1, len(widths))], axis=along))


def rms_parts(value):
    inverse = lax.rsqrt(jnp.mean(value * value, axis=-1, keepdims=True) + EPSILON)
    return (value * inverse, inverse)


def rms_backward(grad_out, scaled, inverse, gain_vec):
    grad_scaled = grad_out * gain_vec
    grad_in = inverse * (
        grad_scaled - scaled * jnp.mean(grad_scaled * scaled, axis=-1, keepdims=True)
    )
    return (grad_in, jnp.sum(grad_out * scaled, axis=0))


def rotate(values_in, position, direction):
    half_dim = values_in.shape[-1] // 2
    inverse = ROPE_BASE ** (-jnp.arange(half_dim, dtype=jnp.float32) / half_dim)
    angles = position.astype(jnp.float32)[:, None] * inverse[None, :]
    cosine = jnp.cos(angles)[:, None, :]
    sine_dir = direction * jnp.sin(angles)[:, None, :]
    front_half = values_in[..., :half_dim]
    back_half = values_in[..., half_dim:]
    return jnp.concatenate(
        [front_half * cosine - back_half * sine_dir, front_half * sine_dir + back_half * cosine],
        axis=-1,
    )


def row_layout(lengths, first_row, amount):
    seq_ends = jnp.cumsum(lengths)
    starts = seq_ends - lengths
    row_ids = first_row + jnp.arange(amount, dtype=jnp.int32)
    segment = jnp.sum((row_ids[:, None] >= seq_ends[None, :]).astype(jnp.int32), axis=1)
    segment = jnp.where(row_ids < 0, jnp.int32(-1), segment)
    picked = segment[:, None] == jnp.arange(lengths.shape[0], dtype=jnp.int32)[None, :]
    begins = jnp.sum(jnp.where(picked, starts[None, :], 0), axis=1)
    return (row_ids, segment, row_ids - begins)


def conv_masks(segment_ext, taps):
    amount = segment_ext.shape[0] - taps + 1
    target = segment_ext[taps - 1 :]
    return jnp.stack(
        [
            (segment_ext[offset : offset + amount] == target).astype(jnp.float32)
            for offset in range(taps)
        ]
    )


def causal_conv(extended, weight, tap_masks):
    amount = extended.shape[0] - weight.shape[0] + 1
    summed = jnp.zeros((amount, extended.shape[1]), jnp.float32)
    for offset in range(weight.shape[0]):
        summed = (
            summed
            + extended[offset : offset + amount]
            * weight[offset][None, :]
            * tap_masks[offset][:, None]
        )
    return summed


def ssm_prepare(x_ext, bc_ext, dt_raw, conv_x, conv_bc, dt_bias, a_log, tap_masks):
    amount = dt_raw.shape[0]
    heads_here = dt_raw.shape[1]
    mixed_x = jax.nn.silu(causal_conv(x_ext, conv_x, tap_masks)).reshape(amount, heads_here, -1)
    mixed_bc = jax.nn.silu(causal_conv(bc_ext, conv_bc, tap_masks))
    state_dim = mixed_bc.shape[1] // 2
    steps_dt = jax.nn.softplus(dt_raw + dt_bias[None, :])
    decay_rate = -jnp.exp(a_log)
    return (mixed_x, mixed_bc[:, :state_dim], mixed_bc[:, state_dim:], steps_dt, decay_rate)


def span_terms(mixed_x, b_rows, c_rows, steps_dt, decay_rate, segment, segment_prev):
    log_decay = steps_dt * decay_rate[None, :]
    cumulative = jnp.cumsum(log_decay, axis=0)
    positions = jnp.arange(segment.shape[0])
    lower_tri = (positions[:, None] >= positions[None, :]) & (segment[:, None] == segment[None, :])
    lower_cube = lower_tri[:, :, None]
    spread = jnp.where(lower_cube, cumulative[:, None, :] - cumulative[None, :, :], 0.0)
    decays = jnp.where(lower_cube, jnp.exp(spread), 0.0)
    inner_cb = jnp.dot(c_rows, b_rows.T, precision=HIGHEST)
    weights = decays * inner_cb[:, :, None] * steps_dt[None, :, :]
    intra_out = jnp.einsum("ijh,jhp->ihp", weights, mixed_x, precision=HIGHEST)
    carried = (segment == segment_prev).astype(jnp.float32)
    entering = jnp.exp(cumulative) * carried[:, None]
    closing = (segment == segment[-1]).astype(jnp.float32)
    to_end = jnp.exp(cumulative[-1][None, :] - cumulative) * closing[:, None] * steps_dt
    span_state = jnp.einsum("jh,jhp,jn->hpn", to_end, mixed_x, b_rows, precision=HIGHEST)
    span_decay = jnp.exp(cumulative[-1]) * (segment[-1] == segment_prev).astype(jnp.float32)
    return (intra_out, entering, span_decay, span_state)


def to_blocks(array_in, blocks):
    return array_in.reshape((blocks, SPAN) + array_in.shape[1:])


def span_all(mixed_x, b_rows, c_rows, steps_dt, decay_rate, segment, segment_prev):
    amount, heads_here, head_dim = mixed_x.shape
    blocks = amount // SPAN
    firsts = segment_prev.reshape(blocks, SPAN)[:, 0]
    intra_out, entering, span_decay, span_state = jax.vmap(
        span_terms, in_axes=(0, 0, 0, 0, None, 0, 0)
    )(
        to_blocks(mixed_x, blocks),
        to_blocks(b_rows, blocks),
        to_blocks(c_rows, blocks),
        to_blocks(steps_dt, blocks),
        decay_rate,
        to_blocks(segment, blocks),
        firsts,
    )

    def compose(running, inputs):
        decay_now, state_now = running
        decay_blk, state_blk = inputs
        return ((decay_now * decay_blk, decay_blk[:, None, None] * state_now + state_blk), None)

    initial = (jnp.ones((heads_here,), jnp.float32), jnp.zeros(span_state.shape[1:], jnp.float32))
    composed, unused = lax.scan(compose, initial, (span_decay, span_state))
    return (intra_out, entering, span_decay, span_state, composed[0], composed[1])


def span_finish(
    state_in, intra_out, entering, span_decay, span_state, c_rows, mixed_x, z_pre, d_skip
):
    blocks = intra_out.shape[0]

    def advance(running, inputs):
        decay_blk, state_blk = inputs
        return (decay_blk[:, None, None] * running + state_blk, running)

    unused, incoming = lax.scan(advance, state_in, (span_decay, span_state))
    c_blocks = c_rows.reshape(blocks, SPAN, -1)
    ssm_out = intra_out + jnp.einsum(
        "cih,cin,chpn->cihp", entering, c_blocks, incoming, precision=HIGHEST
    )
    ssm_out = ssm_out.reshape(mixed_x.shape)
    gated = (ssm_out + d_skip[None, :, None] * mixed_x) * jax.nn.silu(z_pre.reshape(mixed_x.shape))
    return gated.reshape(mixed_x.shape[0], -1)


def chain_forward(earlier, later):
    return (earlier[0] * later[0], later[0][:, None, None] * earlier[1] + later[1])


def chain_backward(earlier, later):
    return (earlier[0] * later[0], later[1] + later[0][:, None, None] * earlier[1])


def keep_block(current):
    return current


def shards(
    x_in,
    lengths,
    norm1_gain,
    w_mix_in,
    w_dt,
    w_shared,
    conv_x,
    conv_bc,
    a_log,
    dt_bias,
    d_skip,
    gate_gain,
    w_out,
    norm2_gain,
    w_gate,
    w_up,
    w_down,
    d_out,
):
    tok_rows = x_in.shape[0]
    groups = lax.axis_size("branch")
    branch_id = lax.axis_index("branch")
    seq_id = lax.axis_index("seq")
    seq_rows = tok_rows * groups
    group_first = seq_id * seq_rows
    att_heads = HEADS_ATT // groups
    att_cols = att_heads * HEAD
    ssm_heads = w_dt.shape[1]
    ssm_cols = ssm_heads * HEAD
    kv_cols = KV * HEAD
    rim_rows = CONV - 1
    att_all = HEADS_ATT * HEAD
    f32 = jnp.float32
    bf16 = jnp.bfloat16
    mix_full, dt_full, shared_full, out_full, gate_full, up_full, down_full = (
        lax.all_gather(w_mix_in, "seq", axis=0, tiled=True),
        lax.all_gather(w_dt, "seq", axis=0, tiled=True),
        lax.all_gather(w_shared, "seq", axis=0, tiled=True),
        lax.all_gather(w_out, "seq", axis=0, tiled=True),
        lax.all_gather(w_gate, "seq", axis=0, tiled=True),
        lax.all_gather(w_up, "seq", axis=0, tiled=True),
        lax.all_gather(w_down, "seq", axis=0, tiled=True),
    )
    x_rows = x_in.astype(f32)
    scaled1, inverse1 = rms_parts(x_rows)
    normed1 = (scaled1 * norm1_gain).astype(bf16)
    group_in = lax.all_gather(normed1, "branch", axis=0, tiled=True)
    row_ids, segment, position = row_layout(lengths, group_first, seq_rows)
    ext_ids, segment_ext, unused_pos = row_layout(
        lengths, group_first - rim_rows, seq_rows + rim_rows
    )
    tap_masks = conv_masks(segment_ext, CONV)
    segment_prev = segment_ext[rim_rows - 1 : rim_rows - 1 + seq_rows]
    kv_head = branch_id * att_heads // (HEADS_ATT // KV)
    key_w = lax.dynamic_slice_in_dim(shared_full, kv_head * HEAD, HEAD, 1)
    value_w = lax.dynamic_slice_in_dim(shared_full, kv_cols + kv_head * HEAD, HEAD, 1)
    side_w = jnp.concatenate([key_w, value_w, shared_full[:, 2 * kv_cols :]], axis=1)
    q_raw = jnp.dot(group_in, mix_full[:, :att_cols], preferred_element_type=f32)
    zx_pre = jnp.dot(group_in, mix_full[:, att_cols:], preferred_element_type=f32)
    dt_raw = jnp.dot(group_in, dt_full, preferred_element_type=f32)
    side_pre = jnp.dot(group_in, side_w, preferred_element_type=f32)
    z_pre = zx_pre[:, :ssm_cols]
    x_pre = zx_pre[:, ssm_cols:]
    bc_pre = side_pre[:, 2 * HEAD :]
    queries = rotate(q_raw.reshape(seq_rows, att_heads, HEAD), position, 1.0).astype(bf16)
    keys_rot = (
        rotate(side_pre[:, :HEAD].reshape(seq_rows, 1, HEAD), position, 1.0)
        .reshape(seq_rows, HEAD)
        .astype(bf16)
    )
    values_b = side_pre[:, HEAD : 2 * HEAD].astype(bf16)
    row_last = group_first + seq_rows - 1
    seq_begin = group_first - position[0]

    def key_visible(first_key, amount):
        key_ids, key_seg, unused = row_layout(lengths, first_key, amount)
        return ((key_ids[None, :] <= row_ids[:, None]) & (key_seg[None, :] == segment[:, None]))[
            :, None, :
        ]

    def reachable(first_key, amount):
        return (first_key <= row_last) & (first_key + amount > seq_begin)

    def over_keys(fold_fn, initial):
        return fold_fn(
            initial,
            (
                lax.all_gather(keys_rot, "seq", axis=0, tiled=True),
                lax.all_gather(values_b, "seq", axis=0, tiled=True),
            ),
            jnp.int32(0),
        )

    def raw_scores(piece_keys):
        return (
            jnp.einsum("rhd,nd->rhn", queries, piece_keys, preferred_element_type=f32) * SCORE_SCALE
        )

    def max_sum(running, pieces, first_key):
        piece_keys, piece_values = pieces
        amount = piece_keys.shape[0]

        def max_compute_block(current):
            top_now, total_now = current
            visible = key_visible(first_key, amount)
            scores = jnp.where(visible, raw_scores(piece_keys), -1e30)
            top_new = jnp.maximum(top_now, jnp.max(scores, axis=-1))
            total_new = jnp.sum(
                jnp.where(visible, jnp.exp(scores - top_new[..., None]), 0.0), axis=-1
            )
            return (top_new, total_new)

        return lax.cond(reachable(first_key, amount), max_compute_block, keep_block, running)

    top_all, total_all = over_keys(
        max_sum,
        (jnp.full((seq_rows, att_heads), -1e30, f32), jnp.zeros((seq_rows, att_heads), f32)),
    )
    log_total = top_all + jnp.log(total_all)

    def probabilities(piece_keys, first_key):
        visible = key_visible(first_key, piece_keys.shape[0])
        return jnp.where(visible, jnp.exp(raw_scores(piece_keys) - log_total[..., None]), 0.0)

    def weighted_values(running, pieces, first_key):
        piece_keys, piece_values = pieces

        def weighted_compute_block(current):
            probs_f = probabilities(piece_keys, first_key)
            probs_b = probs_f.astype(bf16)
            leftover = (probs_f - probs_b.astype(f32)).astype(bf16)
            summed = jnp.einsum("rhn,nd->rhd", probs_b, piece_values, preferred_element_type=f32)
            remainder = jnp.einsum(
                "rhn,nd->rhd", leftover, piece_values, preferred_element_type=f32
            )
            return (summed, remainder)

        return lax.cond(
            reachable(first_key, piece_keys.shape[0]), weighted_compute_block, keep_block, running
        )

    empty3 = jnp.zeros((seq_rows, att_heads, HEAD), f32)
    attn_sum, attn_rest = over_keys(weighted_values, (empty3, empty3))
    attn_out = attn_sum.reshape(seq_rows, att_cols).astype(bf16)
    rim_x, rim_bc = from_behind(
        (x_pre[seq_rows - rim_rows :], bc_pre[seq_rows - rim_rows :]), "seq", 1
    )
    x_ext = jnp.concatenate([rim_x, x_pre], axis=0)
    bc_ext = jnp.concatenate([rim_bc, bc_pre], axis=0)

    def prepare(x_ext, bc_ext, dt_raw, conv_x, conv_bc, dt_bias, a_log):
        return ssm_prepare(x_ext, bc_ext, dt_raw, conv_x, conv_bc, dt_bias, a_log, tap_masks)

    prepared, prepare_back = jax.vjp(
        prepare, x_ext, bc_ext, dt_raw, conv_x, conv_bc, dt_bias, a_log
    )
    mixed_x, b_rows, c_rows, steps_dt, decay_rate = prepared

    def decompose(mixed_x, b_rows, c_rows, steps_dt, decay_rate):
        return span_all(mixed_x, b_rows, c_rows, steps_dt, decay_rate, segment, segment_prev)

    spanned, span_back = jax.vjp(decompose, mixed_x, b_rows, c_rows, steps_dt, decay_rate)
    intra_out, entering, span_decay, span_state, device_decay, device_state = spanned
    chain_identity = (jnp.ones_like(device_decay), jnp.zeros_like(device_state))
    prefix = entering_2((device_decay, device_state), "seq", chain_forward, chain_identity)
    state_in = prefix[1]
    gated_f, finish_back = jax.vjp(
        span_finish,
        state_in,
        intra_out,
        entering,
        span_decay,
        span_state,
        c_rows,
        mixed_x,
        z_pre,
        d_skip,
    )
    gated_b = gated_f.astype(bf16)
    owner_att, owner_ssm = (
        lax.all_to_all(attn_out, "branch", split_axis=0, concat_axis=1, tiled=True),
        lax.all_to_all(gated_b, "branch", split_axis=0, concat_axis=1, tiled=True),
    )
    scaled_g, inverse_g = rms_parts(owner_ssm.astype(f32))
    gated_norm = (scaled_g * gate_gain).astype(bf16)
    projected = jnp.dot(owner_att, out_full[:att_all], preferred_element_type=f32) + jnp.dot(
        gated_norm, out_full[att_all:], preferred_element_type=f32
    )
    middle = x_rows + projected
    scaled2, inverse2 = rms_parts(middle)
    normed2 = (scaled2 * norm2_gain).astype(bf16)
    gate_val = jnp.dot(normed2, gate_full, preferred_element_type=f32)
    up_val = jnp.dot(normed2, up_full, preferred_element_type=f32)
    sig_gate = jax.nn.sigmoid(gate_val)
    silu_gate = gate_val * sig_gate
    hidden = (silu_gate * up_val).astype(bf16)
    y_out = (middle + jnp.dot(hidden, down_full, preferred_element_type=f32)).astype(bf16)
    grad_down = jnp.dot(hidden.T, d_out, preferred_element_type=f32)
    grad_hidden = jnp.dot(d_out, down_full.T, preferred_element_type=f32)
    grad_gate = (grad_hidden * up_val * sig_gate * (1.0 + gate_val * (1.0 - sig_gate))).astype(bf16)
    grad_up = (grad_hidden * silu_gate).astype(bf16)
    grad_w_gate = jnp.dot(normed2.T, grad_gate, preferred_element_type=f32)
    grad_w_up = jnp.dot(normed2.T, grad_up, preferred_element_type=f32)
    grad_normed2 = jnp.dot(grad_gate, gate_full.T, preferred_element_type=f32) + jnp.dot(
        grad_up, up_full.T, preferred_element_type=f32
    )
    grad_middle, grad_n2 = rms_backward(grad_normed2, scaled2, inverse2, norm2_gain)
    grad_middle = grad_middle + d_out.astype(f32)
    grad_proj = grad_middle.astype(bf16)
    grad_w_out = jnp.concatenate(
        [
            jnp.dot(owner_att.T, grad_proj, preferred_element_type=f32),
            jnp.dot(gated_norm.T, grad_proj, preferred_element_type=f32),
        ],
        axis=0,
    )
    grad_att = jnp.dot(grad_proj, out_full[:att_all].T, preferred_element_type=f32).astype(bf16)
    grad_gnormed = jnp.dot(grad_proj, out_full[att_all:].T, preferred_element_type=f32)
    grad_ssm_in, grad_gate_gain = rms_backward(grad_gnormed, scaled_g, inverse_g, gate_gain)
    back_att, back_ssm = (
        lax.all_to_all(grad_att, "branch", split_axis=1, concat_axis=0, tiled=True),
        lax.all_to_all(grad_ssm_in.astype(bf16), "branch", split_axis=1, concat_axis=0, tiled=True),
    )
    (
        grad_state_in,
        grad_intra,
        grad_enter,
        grad_cdecay,
        grad_cstate,
        grad_c_fin,
        grad_x_fin,
        grad_z,
        grad_skip,
    ) = finish_back(back_ssm.astype(f32))
    suffix = entering_3((device_decay, grad_state_in), "seq", chain_backward, chain_identity)
    grad_out_state = suffix[1]
    grad_dev_decay = jnp.sum(grad_out_state * state_in, axis=(1, 2))
    grad_x_span, grad_b, grad_c_span, grad_dt, grad_rate = span_back(
        (grad_intra, grad_enter, grad_cdecay, grad_cstate, grad_dev_decay, grad_out_state)
    )
    grad_x_ext, grad_bc_ext, grad_dt_raw, grad_conv_x, grad_conv_bc, grad_dt_bias, grad_a_log = (
        prepare_back(
            (grad_x_fin + grad_x_span, grad_b, grad_c_fin + grad_c_span, grad_dt, grad_rate)
        )
    )
    rim_back_x, rim_back_bc = from_behind(
        (grad_x_ext[:rim_rows], grad_bc_ext[:rim_rows]), "seq", -1
    )
    grad_x_pre = grad_x_ext[rim_rows:].at[seq_rows - rim_rows :].add(rim_back_x)
    grad_bc_pre = grad_bc_ext[rim_rows:].at[seq_rows - rim_rows :].add(rim_back_bc)
    grad_att_rows = back_att.reshape(seq_rows, att_heads, HEAD)
    delta_rows = jnp.sum(grad_att_rows.astype(f32) * (attn_sum + attn_rest), axis=-1)

    def score_grads(piece_keys, piece_values, first_key):
        probs_f = probabilities(piece_keys, first_key)
        grad_p = jnp.einsum("rhd,nd->rhn", grad_att_rows, piece_values, preferred_element_type=f32)
        return (probs_f, (probs_f * (grad_p - delta_rows[..., None])).astype(bf16))

    seq_ends = jnp.cumsum(lengths)
    last_end = jnp.sum(jnp.where(jnp.arange(lengths.shape[0]) == segment[-1], seq_ends, 0))
    empty_keys = jnp.zeros((seq_rows, HEAD), f32)
    first_row = jnp.int32(0)
    piece_q = lax.all_gather(queries, "seq", axis=0, tiled=True)
    piece_grad = lax.all_gather(grad_att_rows, "seq", axis=0, tiled=True)
    piece_lse = lax.all_gather(log_total.astype(jnp.bfloat16), "seq", axis=0, tiled=True).astype(
        jnp.float32
    )
    piece_delta = lax.all_gather(delta_rows.astype(jnp.bfloat16), "seq", axis=0, tiled=True).astype(
        jnp.float32
    )
    piece_keys = lax.all_gather(keys_rot, "seq", axis=0, tiled=True)
    piece_values = lax.all_gather(values_b, "seq", axis=0, tiled=True)
    amount = piece_q.shape[0]
    grad_q_now = empty3
    grad_k_now = empty_keys
    grad_v_now = empty_keys

    def query_block(current):
        probs_f, grad_s = score_grads(piece_keys, piece_values, first_row)
        return SCORE_SCALE * jnp.einsum(
            "rhn,nd->rhd", grad_s, piece_keys, preferred_element_type=f32
        )

    def key_block(current):
        query_ids, query_seg, unused = row_layout(lengths, first_row, amount)
        visible = (
            (row_ids[None, :] <= query_ids[:, None]) & (segment[None, :] == query_seg[:, None])
        )[:, None, :]
        scores = (
            jnp.einsum("nhd,rd->nhr", piece_q, keys_rot, preferred_element_type=f32) * SCORE_SCALE
        )
        probs_f = jnp.where(visible, jnp.exp(scores - piece_lse[..., None]), 0.0)
        grad_p = jnp.einsum("nhd,rd->nhr", piece_grad, values_b, preferred_element_type=f32)
        grad_s = (probs_f * (grad_p - piece_delta[..., None])).astype(bf16)
        grad_k = SCORE_SCALE * jnp.einsum(
            "nhr,nhd->rd", grad_s, piece_q, preferred_element_type=f32
        )
        grad_v = jnp.einsum(
            "nhr,nhd->rd", probs_f.astype(bf16), piece_grad, preferred_element_type=f32
        )
        return (grad_k, grad_v)

    grad_q_now = lax.cond(reachable(first_row, amount), query_block, keep_block, grad_q_now)
    near_enough = (first_row + amount > group_first) & (first_row < last_end)
    grad_k_now, grad_v_now = lax.cond(near_enough, key_block, keep_block, (grad_k_now, grad_v_now))
    grad_q_raw = rotate(grad_q_now, position, -1.0).reshape(seq_rows, att_cols).astype(bf16)
    grad_k_raw = rotate(grad_k_now.reshape(seq_rows, 1, HEAD), position, -1.0).reshape(
        seq_rows, HEAD
    )
    grad_side = jnp.concatenate([grad_k_raw, grad_v_now, grad_bc_pre], axis=1)
    grad_zx = jnp.concatenate([grad_z, grad_x_pre], axis=1).astype(bf16)
    grad_dt_b = grad_dt_raw.astype(bf16)
    grad_group = (
        jnp.dot(grad_q_raw, mix_full[:, :att_cols].T, preferred_element_type=f32)
        + jnp.dot(grad_zx, mix_full[:, att_cols:].T, preferred_element_type=f32)
        + jnp.dot(grad_dt_b, dt_full.T, preferred_element_type=f32)
        + jnp.dot(grad_side, side_w.astype(f32).T, precision=HIGHEST)
    )
    grad_normed1 = lax.psum_scatter(
        grad_group.astype(jnp.bfloat16), "branch", scatter_dimension=0, tiled=True
    ).astype(jnp.float32)
    grad_x1, grad_n1 = rms_backward(grad_normed1, scaled1, inverse1, norm1_gain)
    grad_x_rows = grad_middle + grad_x1
    grad_mix = jnp.concatenate(
        [
            jnp.dot(group_in.T, grad_q_raw, preferred_element_type=f32),
            jnp.dot(group_in.T, grad_zx, preferred_element_type=f32),
        ],
        axis=1,
    )
    grad_dt_w = jnp.dot(group_in.T, grad_dt_b, preferred_element_type=f32)
    grad_side_w = jnp.dot(group_in.astype(f32).T, grad_side, precision=HIGHEST)
    kv_pick = (jnp.arange(KV) == kv_head).astype(f32)
    width_rows = grad_side_w.shape[0]
    grad_shared = jnp.concatenate(
        [
            (grad_side_w[:, None, :HEAD] * kv_pick[None, :, None]).reshape(width_rows, kv_cols),
            (grad_side_w[:, None, HEAD : 2 * HEAD] * kv_pick[None, :, None]).reshape(
                width_rows, kv_cols
            ),
            grad_side_w[:, 2 * HEAD :],
        ],
        axis=1,
    )
    reduced = (
        lax.psum_scatter(grad_n1, ("branch", "seq"), scatter_dimension=0, tiled=True),
        lax.psum_scatter(grad_shared, ("branch", "seq"), scatter_dimension=0, tiled=True),
        lax.psum_scatter(grad_conv_bc, ("branch", "seq"), scatter_dimension=1, tiled=True),
        lax.psum_scatter(grad_gate_gain, ("branch", "seq"), scatter_dimension=0, tiled=True),
        lax.psum_scatter(grad_w_out, ("branch", "seq"), scatter_dimension=0, tiled=True),
        lax.psum_scatter(grad_n2, ("branch", "seq"), scatter_dimension=0, tiled=True),
        lax.psum_scatter(grad_w_gate, ("branch", "seq"), scatter_dimension=0, tiled=True),
        lax.psum_scatter(grad_w_up, ("branch", "seq"), scatter_dimension=0, tiled=True),
        lax.psum_scatter(grad_down, ("branch", "seq"), scatter_dimension=0, tiled=True),
    )
    branch_red = (
        *side_by_side((grad_mix.astype(jnp.bfloat16), grad_dt_w.astype(jnp.bfloat16)), "seq", 0, 1),
        sent_and_summed(grad_conv_x.astype(jnp.bfloat16), "seq", 1),
    )
    head_red = lax.psum((grad_a_log, grad_dt_bias, grad_skip), "seq")
    return (
        y_out,
        grad_x_rows,
        reduced[0],
        branch_red[0],
        branch_red[1],
        reduced[1],
        branch_red[2],
        reduced[2],
        head_red[0],
        head_red[1],
        head_red[2],
        reduced[3],
        reduced[4],
        reduced[5],
        reduced[6],
        reduced[7],
        reduced[8],
    )


def solution(mesh):
    in_specs = (
        P(("seq", "branch"), None),
        P(),
        P(),
        P("seq", "branch"),
        P("seq", "branch"),
        P("seq", None),
        P(None, "branch"),
        P(),
        P("branch"),
        P("branch"),
        P("branch"),
        P(),
        P("seq", None),
        P(),
        P("seq", None),
        P("seq", None),
        P("seq", None),
        P(("seq", "branch"), None),
    )
    out_specs = (
        P(("seq", "branch"), None),
        P(("seq", "branch"), None),
        P(("branch", "seq")),
        P("seq", "branch"),
        P("seq", "branch"),
        P(("branch", "seq"), None),
        P(None, ("branch", "seq")),
        P(None, ("branch", "seq")),
        P("branch"),
        P("branch"),
        P("branch"),
        P(("branch", "seq")),
        P(("branch", "seq"), None),
        P(("branch", "seq")),
        P(("branch", "seq"), None),
        P(("branch", "seq"), None),
        P(("branch", "seq"), None),
    )
    return jax.shard_map(shards, mesh=mesh, in_specs=in_specs, out_specs=out_specs, check_vma=False)
```

profile of v0, /device:TPU:4, one launch (start us, length us, event | category | flops | bytes accessed | tf_op | source)
XLA Modules:
  0.0 1336.0 jit_solution(7514429778717044723)
XLA Ops:
  16.1 13.1 all_gather.71
  43.6 18.6 %all-gather.18.cloned.1.call-done = bf16[1024,512]{1,0:T(8,128)(2,1)} async-done(((bf16[128,512]{1,0:T(8,128)(2,1)}), bf16[1024,512]{1,0:T(8,128)(2,1)}) %all-gather.18.cloned.1.call-update) | async-done | bytes 1048592 | tf_op jit(solution)/shard_map/all_gather | solution.py:282
  69.0 18.0 %all-gather = bf16[4096,1,64]{0,2,1:T(8,128)(2,1)} all-gather(bf16[512,1,64]{0,2,1:T(8,128)(2,1)S(1)} %get-tuple-element.1415), channel_id=2, replica_groups=mesh['branch'=4,'seq'=8] {'seq'}, dimensions={0}, use_global_device_ids=true | all-gather | bytes 589824 | tf_op jit(solution)/shard_map/all_gather | solution.py:332
  87.0 19.3 %all_gather.69 = bf16[4096,64]{1,0:T(8,128)(2,1)} all-gather(bf16[512,64]{1,0:T(8,128)(2,1)S(1)} %slice.423), channel_id=1, replica_groups=mesh['branch'=4,'seq'=8] {'seq'}, dimensions={0}, use_global_device_ids=true | all-gather | bytes 589824 | tf_op jit(solution)/shard_map/all_gather | solution.py:333
  126.4 14.0 %all-reduce.20 = bf16[48]{0:T(256)(128)(2,1)S(1)} all-reduce(bf16[48]{0:T(256)(128)(2,1)S(1)} %dynamic-update-slice.6), channel_id=3, replica_groups=mesh['branch'=4,'seq'=8] {'seq'}, use_global_device_ids=true, to_apply=%add.20 | all-reduce | flops 48 | bytes 192
  140.5 16.8 %all-gather.2 = bf16[48,64,128]{2,1,0:T(8,128)(2,1)} all-gather(bf16[6,64,128]{2,1,0:T(8,128)(2,1)S(1)} %convert_element_type.302), channel_id=4, replica_groups=mesh['branch'=4,'seq'=8] {'seq'}, dimensions={0}, use_global_device_ids=true | all-gather | bytes 884736 | tf_op jit(solution)/shard_map/all_gather | solution.py:28
  190.2 16.1 %conditional.4 = (f32[512,2]{0,1:T(2,128)}, f32[512,2]{0,1:T(2,128)S(1)}) conditional(s32[]{:T(128)} %convert_element_type.289, () %tuple.158, (s32[512]{0:T(512)}, s32[5]{0:T(128)}, s32[512]{0:T(512)}, bf16[512,2,64]{0,2,1:T(8,128)(2,1)}, bf16[4096,64]{0,1:T(8,128)(2,1)S(1)}) %tuple.418), branch_computations={%region_4.5_spmd, %region_5.10_spmd} | conditional | flops 576773120 | bytes 40566864 | solution.py:357
  207.6 32.3 %conditional.5 = (f32[512,2,64]{0,2,1:T(8,128)}, f32[512,2,64]{0,2,1:T(8,128)}) conditional(s32[]{:T(128)} %convert_element_type.289, () %tuple.157, (s32[512]{0:T(512)}, s32[5]{0:T(128)}, s32[512]{0:T(512)}, bf16[512,2,64]{0,2,1:T(8,128)(2,1)}, bf16[4096,64]{0,1:T(8,128)(2,1)S(1)}, /*index=5*/f32[512,2]{0,1:T(2,128)}, ...), branch_computations={%region_10.11_spmd, %region_11.14_spmd} | conditional | flops 1663098880 | bytes 111341800 | solution.py:382
  320.7 32.0 %conditional.6 = (f32[512,2,32]{0,2,1:T(8,128)S(1)}, f32[512,2,32]{0,2,1:T(8,128)S(1)}) conditional(s32[]{:T(128)} %convert_element_type.289, () %tuple.164, (s32[512]{0:T(512)}, s32[5]{0:T(128)}, s32[512]{0:T(512)}, bf16[512,2,64]{0,2,1:T(8,128)(2,1)}, bf16[4096,64]{0,1:T(8,128)(2,1)}, /*index=5*/f32[512,2]{0,1:T(2,128)}, ...), branch_computations={%region_26.27_spmd, %region_27.30_spmd} | conditional | flops 1642192896 | bytes 40415312 | solution.py:547
  336.2 15.4 %fusion.24 = f32[512,2,64]{0,2,1:T(8,128)} fusion(f32[512,2,4096]{2,0,1:T(8,128)} %fusion.28, bf16[512,2,64]{0,2,1:T(8,128)(2,1)} %get-tuple-element.727, f32[512,2]{0,1:T(2,128)} %get-tuple-element.729, f32[512,2]{0,1:T(2,128)} %get-tuple-element.726, pred[512,4096]{1,0:T(8,128)(4,1)} %fusion.22, bf16[4096,64]{1,0:T(8,128)(2,1)} %get-tuple-element.1209, ...), kind=kOutput, calls=%fused_computation.40 | convolution fusion | flops 1098973184 | bytes 20324352 | tf_op jit(solution)/shard_map/cond/branch_1_fun/rhn,nd->rhd/dot_general | solution.py:524
  354.2 13.1 all_gather.84
  386.5 16.7 %while.108 = (s32[]{:T(128)}, f32[6,64,128]{2,1,0:T(8,128)S(1)}, f32[4,6]{1,0:T(4,128)}, f32[4,6,64,128]{3,2,1,0:T(8,128)}, f32[4,6,64,128]{3,2,1,0:T(8,128)}, /...) while((s32[]{:T(128)}, f32[6,64,128]{2,1,0:T(8,128)S(1)}, ...), condition=%wide.region_33.34_spmd.clone, body=%wide.region_31.33_spmd.clone.sunk | while | flops 294910 | bytes 1179940 | solution.py:222
  403.2 17.2 %all-gather.3 = bf16[48,64,128]{2,1,0:T(8,128)(2,1)} all-gather(bf16[6,64,128]{2,1,0:T(8,128)(2,1)S(1)} %convert_element_type.325), channel_id=5, replica_groups=mesh['branch'=4,'seq'=8] {'seq'}, dimensions={0}, use_global_device_ids=true | all-gather | bytes 884736 | tf_op jit(solution)/shard_map/all_gather | solution.py:51
  420.4 17.8 %while.109 = (s32[]{:T(128)}, f32[6,64,128]{2,1,0:T(8,128)S(1)}, s32[]{:T(128)}, bf16[8,6,64,128]{3,2,1,0:T(8,128)(2,1)}, bf16[8,6]{1,0:T(8,128)(2,1)}, /*index=5*/s32[]{:T(128)}, s32[]{:T(128)}, s32[]{:T(128)}, s32[]{:T(128)}) while((s32[]{:T(128)}, f32[6,64,128]{2,1,0:T(8,128)S(1)}, s32[]{:T(128)}, ...), condition=%wide.region_35.36_spmd.clone, body=%wide.region_34.35_spmd.clone.sunk | while | flops 245774 | bytes 491755 | solution.py:69
  439.9 14.7 %while.105 = (s32[]{:T(128)}, f32[6]{0:T(128)}, f32[6,64,128]{2,1,0:T(8,128)S(1)}, f32[4,6]{1,0:T(4,128)S(1)}, f32[4,6,64,128]{3,2,1,0:T(8,128)}, /*index=5*/f32...) while((s32[]{:T(128)}, f32[6]{0:T(128)}, ...), condition=%wide.region_39.40_spmd, body=%wide.region_37.39_spmd.sunk | while | flops 147471 | bytes 983485 | solution.py:209
  505.8 37.9 %conditional.7 = (f32[512,1,32]{0,2,1:T(8,128)S(1)}, f32[512,1,32]{0,2,1:T(8,128)S(1)}, f32[512,64]{1,0:T(8,128)S(1)}) conditional(s32[]{:T(128)} %convert_element_type.327, () %tuple.169, (s32[512]{0:T(512)S(1)}, s32[512]{0:T(512)S(1)}, s32[5]{0:T(128)S(1)}, bf16[4096,2,64]{0,2,1:T(8,128)(2,1)}, bf16[512,64]{0,1:T(8,128)(2,1)S(1)}, ...), branch_computations={%region_46.47_spmd, %region_47.50_spmd} | conditional | flops 2195808256 | bytes 61608024 | solution.py:549
  518.8 14.2 %fusion.51 = f32[512,1,64]{0,2,1:T(8,128)S(1)} fusion(bf16[4096,2,64]{0,2,1:T(8,128)(2,1)} %get-tuple-element.757, f32[4096,2,512]{2,0,1:T(8,128)} %fusion.54, bf16[4096,2,64]{0,2,1:T(8,128)(2,1)} %get-tuple-element.760, f32[4096,2]{0,1:T(2,128)S(1)} %get-tuple-element.762, f32[4096,2]{0,1:T(2,128)S(1)} %get-tuple-element.759, ...), kind=kOutput, calls=%fused_computation.74 | convolution fusion | flops 1098940416 | bytes 21233664 | tf_op jit(solution)/shard_map/cond/branch_1_fun/nhr,nhd->rd/dot_general | solution.py:539
  600.4 44.7 %all-reduce.26 = (f32[6]{0:T(128)}, f32[6]{0:T(128)}, f32[6]{0:T(128)}) all-reduce(f32[6]{0:T(128)S(1)} %negate_multiply_fusion, f32[6]{0:T(128)S(1)} %get-tuple-element.1353, f32[6]{0:T(128)S(1)} %reduce_sum.492), channel_id=1, replica_groups=mesh['branch'=4,'seq'=8] {'seq'}, use_global_device_ids=true, to_apply=%region_68.69 | all-reduce | flops 18 | bytes 144 | tf_op jit(solution)/shard_map/psum | solution.py:604
  653.4 47.4 %all-reduce.25 = (f32[1024]{0:T(1024)S(1)}, f32[4,256]{1,0:T(4,128)S(1)}, f32[1536]{0:T(1024)S(1)}, f32[1024]{0:T(1024)S(1)}) all-reduce(f32[1024]{0:T(1024)S(1)} %get-tuple-element.1257, f32[4,256]{1,0:T(4,128)S(1)} %pad_add_fusion.4, f32[1536]{0:T(1024)S(1)} %copy-done.137, ...), channel_id=7, replica_groups=mesh['branch'=4,'seq'=8] {'branch','seq'}, use_global_device_ids=true, to_apply=%region_54.55.clone | all-reduce | flops 4608 | bytes 36864
  705.3 15.6 %reduce-scatter.20.cloned.1.call-done = f32[32,512]{1,0:T(8,128)} async-done(((f32[1024,512]{1,0:T(8,128)}), f32[32,512]{1,0:T(8,128)}) %reduce-scatter.20.cloned.1.call-update) | async-done | bytes 65552
  720.8 151.2 %reduce-scatter.12.cloned.1.call-done = f32[64,1024]{1,0:T(8,128)} async-done(((f32[2048,1024]{1,0:T(8,128)}), f32[64,1024]{1,0:T(8,128)}) %reduce-scatter.12.cloned.1.call-update) | async-done | bytes 262160 | tf_op jit(solution)/shard_map/reduce_scatter | solution.py:594
  872.0 152.7 %reduce-scatter.14.cloned.1.call-done = f32[32,2048]{1,0:T(8,128)} async-done(((f32[1024,2048]{1,0:T(8,128)}), f32[32,2048]{1,0:T(8,128)}) %reduce-scatter.14.cloned.1.call-update) | async-done | bytes 262160 | tf_op jit(solution)/shard_map/reduce_scatter | solution.py:596
  1024.7 152.9 %reduce-scatter.16.cloned.1.call-done = f32[32,2048]{1,0:T(8,128)} async-done(((f32[1024,2048]{1,0:T(8,128)}), f32[32,2048]{1,0:T(8,128)}) %reduce-scatter.16.cloned.1.call-update) | async-done | bytes 262160 | tf_op jit(solution)/shard_map/reduce_scatter | solution.py:597
  1177.6 151.6 %reduce-scatter.18.cloned.1.call-done = f32[64,1024]{1,0:T(8,128)} async-done(((f32[2048,1024]{1,0:T(8,128)}), f32[64,1024]{1,0:T(8,128)}) %reduce-scatter.18.cloned.1.call-update) | async-done | bytes 262160 | tf_op jit(solution)/shard_map/reduce_scatter | solution.py:598
  (762 shorter events, 455.9 us)
Async XLA Ops:
  7.3 31.1 %all-gather.14.cloned.1.call-start = ((), (), s32[]{:S(2)}) async-start(), calls=%async_computation.12 | async-start | bytes 1310720 | tf_op jit(solution)/shard_map/all_gather | solution.py:291
  10.2 51.9 %all-gather.18.cloned.1.call-start = ((), (), s32[]{:S(2)}) async-start(), calls=%async_computation.14 | async-start | bytes 1179648 | tf_op jit(solution)/shard_map/all_gather | solution.py:282
  11.0 98.8 %all-gather.16.cloned.1.call-start = ((), (), s32[]{:S(2)}) async-start(), calls=%async_computation.13 | async-start | bytes 2064384 | tf_op jit(solution)/shard_map/all_gather | solution.py:280
  11.7 255.7 %all-gather.20.cloned.1.call-start = ((), (), s32[]{:S(2)}) async-start(), calls=%async_computation.15 | async-start | bytes 4718592 | tf_op jit(solution)/shard_map/all_gather | solution.py:283
  12.3 263.3 %all-gather.22.cloned.1.call-start = ((), (), s32[]{:S(2)}) async-start(), calls=%async_computation.16 | async-start | bytes 4718592 | tf_op jit(solution)/shard_map/all_gather | solution.py:284
  12.9 266.8 %all-gather.24.cloned.1.call-start = ((), (), s32[]{:S(2)}) async-start(), calls=%async_computation.17 | async-start | bytes 4718592 | tf_op jit(solution)/shard_map/all_gather | solution.py:285
  13.5 273.8 %all-gather.26.cloned.1.call-start = ((), (), s32[]{:S(2)}) async-start(), calls=%async_computation.18 | async-start | bytes 4718592 | tf_op jit(solution)/shard_map/all_gather | solution.py:286
  65.7 40.6 %collective-permute-start.1 = (f32[3,256]{1,0:T(4,128)S(1)}, f32[3,256]{1,0:T(4,128)S(1)}, u32[]{:S(2)}, u32[]{:S(2)}) collective-permute-start(f32[3,256]{1,0:T(4,128)S(1)} %slice.303), channel_id=1, source_target_pairs={{0,1},{1,2},{2,3},{3,4},{4,5},{5,6},{6,7},{8,9},{9,10},{10,11},{11... | collective-permute-start | bytes 9224 | tf_op jit(solution)/shard_map/ppermute | solution.py:22
  112.3 4.5 collective-permute-start
  183.8 76.0 %all-to-all-start.1 = ((bf16[4,128,384]{2,1,0:T(8,128)(2,1)}), bf16[4,128,384]{2,1,0:T(8,128)(2,1)}, u32[]{:S(2)}, u32[]{:S(2)}) async-start(bf16[4,128,384]{2,1,0:T(8,128)(2,1)} %bitcast.405), calls=%async_computation.1 | async-start | bytes 786432 | tf_op jit(solution)/shard_map/all_to_all | solution.py:426
  188.6 317.0 %all-gather.28.cloned.1.call-start = ((), (), s32[]{:S(2)}) async-start(), calls=%async_computation.19 | async-start | bytes 1179648 | tf_op jit(solution)/shard_map/all_gather | solution.py:507
  259.8 11.2 all-to-all-start
  301.8 9.6 all-to-all-start.2
  311.4 59.3 %all-to-all-start.3 = ((bf16[128,4,384]{2,0,1:T(8,128)(2,1)}), bf16[128,4,384]{2,0,1:T(8,128)(2,1)}, u32[]{:S(2)}, u32[]{:S(2)}) async-start(bf16[128,4,384]{2,0,1:T(8,128)(2,1)} %bitcast.406), calls=%async_computation.3 | async-start | bytes 786432 | tf_op jit(solution)/shard_map/all_to_all | solution.py:466
  315.6 190.1 %all-gather.30.cloned.1.call-start = ((), (), s32[]{:S(2)}) async-start(), calls=%async_computation.20 | async-start | bytes 1179648 | tf_op jit(solution)/shard_map/all_gather | solution.py:508
  320.6 331.5 %reduce-scatter.10.cloned.1.call-start = ((), (), s32[]{:S(2)}) async-start(), calls=%async_computation.21 | async-start | bytes 1310720 | tf_op jit(solution)/shard_map/reduce_scatter | solution.py:563
  487.3 10.8 collective-permute-start.3
  550.3 170.6 %reduce-scatter.20.cloned.1.call-start = ((), (), s32[]{:S(2)}) async-start(), calls=%async_computation.26 | async-start | bytes 2162688
  556.7 315.3 %reduce-scatter.12.cloned.1.call-start = ((), (), s32[]{:S(2)}) async-start(), calls=%async_computation.22 | async-start | bytes 8650752 | tf_op jit(solution)/shard_map/reduce_scatter | solution.py:594
  562.6 462.1 %reduce-scatter.14.cloned.1.call-start = ((), (), s32[]{:S(2)}) async-start(), calls=%async_computation.23 | async-start | bytes 8650752 | tf_op jit(solution)/shard_map/reduce_scatter | solution.py:596
  568.3 609.3 %reduce-scatter.16.cloned.1.call-start = ((), (), s32[]{:S(2)}) async-start(), calls=%async_computation.24 | async-start | bytes 8650752 | tf_op jit(solution)/shard_map/reduce_scatter | solution.py:597
  574.0 755.2 %reduce-scatter.18.cloned.1.call-start = ((), (), s32[]{:S(2)}) async-start(), calls=%async_computation.25 | async-start | bytes 8650752 | tf_op jit(solution)/shard_map/reduce_scatter | solution.py:598
  581.6 10.5 all-to-all-start.5
  592.1 56.6 %all-to-all-start.4 = ((bf16[8,128,902]{1,2,0:T(8,128)(2,1)}), bf16[8,128,902]{1,2,0:T(8,128)(2,1)}, u32[]{:S(2)}, u32[]{:S(2)}) async-start(bf16[8,128,902]{1,2,0:T(8,128)(2,1)} %copy.359), calls=%async_computation.5 | async-start | bytes 3702784 | tf_op jit(solution)/shard_map/all_to_all | solution.py:79
  (172 other events, 3136.5 us)
Sparse Core Ops, SparseCore 0:
  10.5 27.7 all-gather.13
  40.0 22.1 all-gather.17
  63.8 32.5 all-gather.15
  97.9 47.4 all-gather.19
  146.8 45.5 all-gather.21
  193.9 45.8 all-gather.23
  241.4 45.8 all-gather.25
  288.9 21.0 all-gather.27
  320.7 20.7 all-gather.29
  550.4 28.6 reduce-scatter.9
  582.1 138.7 reduce-scatter.19
  723.6 148.4 reduce-scatter.11
  874.9 149.7 reduce-scatter.13
  1027.4 150.1 reduce-scatter.15
  1180.3 148.8 reduce-scatter.17
where the time goes:
time: 1350 us; the launch traced here: 1340 us
  waiting for transfers between devices  655 us (49%)
  blocking collectives  217 us (16%)
  matrix products  191 us (14%)
  other arithmetic  140 us (10%)
  local copies, waits for them, and re-layouts  78.7 us (6%)
  starting transfers between devices  34.6 us (3%)
  between operations  18.8 us (1%)
    reduce_scatter x1, waiting for transfers between devices, shards(): lax.psum_scatter(grad_w_up, ('branch', 'seq'), scatter_dimension=0, tiled...  153 us
    reduce_scatter x1, waiting for transfers between devices, shards(): lax.psum_scatter(grad_w_gate, ('branch', 'seq'), scatter_dimension=0, til...  153 us
    reduce_scatter x1, waiting for transfers between devices, shards(): lax.psum_scatter(grad_down, ('branch', 'seq'), scatter_dimension=0, tiled...  152 us
    reduce_scatter x1, waiting for transfers between devices, shards(): lax.psum_scatter(grad_w_out, ('branch', 'seq'), scatter_dimension=0, tile...  151 us
    unnamed x2, blocking collectives  61.4 us
    psum x1, blocking collectives, shards(): head_red = lax.psum((grad_a_log, grad_dt_bias, grad_skip), 'seq')  44.7 us
  transfers between devices with their start and end apart: 25, of which 11 were waited for; matrix products, arithmetic and copies ran while one was open for 26% of the time, Pallas kernels for 0%

commit v1 on v0

--- a/solution.py
+++ b/solution.py
@@ -276,36 +276,102 @@
     att_all = HEADS_ATT * HEAD
     f32 = jnp.float32
     bf16 = jnp.bfloat16
-    mix_full, dt_full, shared_full, out_full, gate_full, up_full, down_full = (
-        lax.all_gather(w_mix_in, "seq", axis=0, tiled=True),
-        lax.all_gather(w_dt, "seq", axis=0, tiled=True),
-        lax.all_gather(w_shared, "seq", axis=0, tiled=True),
-        lax.all_gather(w_out, "seq", axis=0, tiled=True),
-        lax.all_gather(w_gate, "seq", axis=0, tiled=True),
-        lax.all_gather(w_up, "seq", axis=0, tiled=True),
-        lax.all_gather(w_down, "seq", axis=0, tiled=True),
-    )
+    dim = x_in.shape[1]
+    parts = lax.axis_size("seq")
+    chunk = w_out.shape[0] // groups
+    att_chunks = parts * att_cols // (att_cols + ssm_cols)
+    ssm_chunks = parts - att_chunks
+    strip = dim // (groups * parts)
+    hidden_all = w_gate.shape[1]
+    hidden_a = hidden_all * att_cols // ((att_cols + ssm_cols) * groups)
+    hidden_s = hidden_all // groups - hidden_a
+    hidden_b = hidden_a + hidden_s
+
+    def spot(c):
+        first = groups * att_chunks
+        if c < first:
+            return (c // att_chunks) * parts + c % att_chunks
+        return ((c - first) // ssm_chunks) * parts + att_chunks + (c - first) % ssm_chunks
+
+    to_heads = [((c % groups) * parts + c // groups, spot(c)) for c in range(groups * parts)]
+    from_heads = [(spot(c), c) for c in range(groups * parts)]
+
+    def branch_sum(part):
+        total = part
+        for k in range(1, groups):
+            route = [(i, (i + k) % groups) for i in range(groups)]
+            total = total + lax.ppermute(part, "branch", route)
+        return total
+
+    def branch_gather(part):
+        copies = jnp.broadcast_to(part[None], (groups,) + part.shape)
+        return lax.all_to_all(copies, "branch", 0, 0, tiled=True).reshape(
+            (groups * part.shape[0],) + part.shape[1:]
+        )
+
+    def branch_scatter(terms):
+        blocks = terms.astype(bf16).reshape((groups, -1) + terms.shape[1:])
+        return jnp.sum(lax.all_to_all(blocks, "branch", 0, 0, tiled=True).astype(f32), axis=0)
+
+    kv_head = branch_id * att_heads // (HEADS_ATT // KV)
+    dt_pad = 128
+    w1_part = jnp.concatenate(
+        [
+            w_mix_in[:, :att_cols],
+            lax.dynamic_slice_in_dim(w_shared, kv_head * HEAD, HEAD, 1),
+            lax.dynamic_slice_in_dim(w_shared, kv_cols + kv_head * HEAD, HEAD, 1),
+            w_mix_in[:, att_cols:],
+            w_shared[:, 2 * kv_cols :],
+            jnp.pad(w_dt, ((0, 0), (0, dt_pad - ssm_heads))),
+        ],
+        axis=1,
+    )
+    w1 = lax.all_gather(w1_part, "seq", axis=0, tiled=True)
+
+    def own_columns(w):
+        return [
+            lax.dynamic_slice_in_dim(w, branch_id * hidden_a, hidden_a, 1),
+            lax.dynamic_slice_in_dim(w, groups * hidden_a + branch_id * hidden_s, hidden_s, 1),
+        ]
+
+    row_part = jnp.concatenate(
+        [
+            lax.dynamic_slice_in_dim(w_out, branch_id * chunk, chunk, 0),
+            lax.dynamic_slice_in_dim(w_down, branch_id * chunk, chunk, 0),
+        ],
+        axis=0,
+    )
+    row_part = lax.ppermute(row_part, ("branch", "seq"), to_heads)
+    w2_part = jnp.concatenate(
+        [row_part, jnp.concatenate(own_columns(w_gate) + own_columns(w_up), axis=1)], axis=0
+    )
+    w2 = lax.all_gather(w2_part, "seq", axis=0)
+    w_out_b = w2[:, :chunk].reshape(parts * chunk, dim)
+    w_down_b = w2[:, chunk : 2 * chunk].reshape(parts * chunk, dim)
+    w_gu = w2[:, 2 * chunk :].reshape(dim, 2 * hidden_b)
     x_rows = x_in.astype(f32)
     scaled1, inverse1 = rms_parts(x_rows)
     normed1 = (scaled1 * norm1_gain).astype(bf16)
-    group_in = lax.all_gather(normed1, "branch", axis=0, tiled=True)
+    group_in = branch_gather(normed1)
+    d_out_g = branch_gather(d_out)
     row_ids, segment, position = row_layout(lengths, group_first, seq_rows)
     ext_ids, segment_ext, unused_pos = row_layout(
         lengths, group_first - rim_rows, seq_rows + rim_rows
     )
     tap_masks = conv_masks(segment_ext, CONV)
     segment_prev = segment_ext[rim_rows - 1 : rim_rows - 1 + seq_rows]
-    kv_head = branch_id * att_heads // (HEADS_ATT // KV)
-    key_w = lax.dynamic_slice_in_dim(shared_full, kv_head * HEAD, HEAD, 1)
-    value_w = lax.dynamic_slice_in_dim(shared_full, kv_cols + kv_head * HEAD, HEAD, 1)
-    side_w = jnp.concatenate([key_w, value_w, shared_full[:, 2 * kv_cols :]], axis=1)
-    q_raw = jnp.dot(group_in, mix_full[:, :att_cols], preferred_element_type=f32)
-    zx_pre = jnp.dot(group_in, mix_full[:, att_cols:], preferred_element_type=f32)
-    dt_raw = jnp.dot(group_in, dt_full, preferred_element_type=f32)
-    side_pre = jnp.dot(group_in, side_w, preferred_element_type=f32)
-    z_pre = zx_pre[:, :ssm_cols]
-    x_pre = zx_pre[:, ssm_cols:]
-    bc_pre = side_pre[:, 2 * HEAD :]
+    pre = jnp.dot(group_in, w1, preferred_element_type=f32)
+    at_k = att_cols
+    at_z = at_k + 2 * HEAD
+    at_x = at_z + ssm_cols
+    at_bc = at_x + ssm_cols
+    at_dt = at_bc + w_shared.shape[1] - 2 * kv_cols
+    q_raw = pre[:, :at_k]
+    side_pre = pre[:, at_k:at_z]
+    z_pre = pre[:, at_z:at_x]
+    x_pre = pre[:, at_x:at_bc]
+    bc_pre = pre[:, at_bc:at_dt]
+    dt_raw = pre[:, at_dt : at_dt + ssm_heads]
     queries = rotate(q_raw.reshape(seq_rows, att_heads, HEAD), position, 1.0).astype(bf16)
     keys_rot = (
         rotate(side_pre[:, :HEAD].reshape(seq_rows, 1, HEAD), position, 1.0)
@@ -325,15 +391,13 @@
     def reachable(first_key, amount):
         return (first_key <= row_last) & (first_key + amount > seq_begin)
 
+    kv_all = lax.all_gather(
+        jnp.concatenate([keys_rot, values_b], axis=1), "seq", axis=0, tiled=True
+    )
+    piece_keys, piece_values = (kv_all[:, :HEAD], kv_all[:, HEAD:])
+
     def over_keys(fold_fn, initial):
-        return fold_fn(
-            initial,
-            (
-                lax.all_gather(keys_rot, "seq", axis=0, tiled=True),
-                lax.all_gather(values_b, "seq", axis=0, tiled=True),
-            ),
-            jnp.int32(0),
-        )
+        return fold_fn(initial, (piece_keys, piece_values), jnp.int32(0))
 
     def raw_scores(piece_keys):
         return (
@@ -386,9 +450,8 @@
     empty3 = jnp.zeros((seq_rows, att_heads, HEAD), f32)
     attn_sum, attn_rest = over_keys(weighted_values, (empty3, empty3))
     attn_out = attn_sum.reshape(seq_rows, att_cols).astype(bf16)
-    rim_x, rim_bc = from_behind(
-        (x_pre[seq_rows - rim_rows :], bc_pre[seq_rows - rim_rows :]), "seq", 1
-    )
+    rim = from_behind(pre[seq_rows - rim_rows :, at_x:at_dt], "seq", 1)
+    rim_x, rim_bc = (rim[:, :ssm_cols], rim[:, ssm_cols:])
     x_ext = jnp.concatenate([rim_x, x_pre], axis=0)
     bc_ext = jnp.concatenate([rim_bc, bc_pre], axis=0)
 
@@ -421,50 +484,82 @@
         d_skip,
     )
     gated_b = gated_f.astype(bf16)
-    owner_att, owner_ssm = (
-        lax.all_to_all(attn_out, "branch", split_axis=0, concat_axis=1, tiled=True),
-        lax.all_to_all(gated_b, "branch", split_axis=0, concat_axis=1, tiled=True),
-    )
-    scaled_g, inverse_g = rms_parts(owner_ssm.astype(f32))
-    gated_norm = (scaled_g * gate_gain).astype(bf16)
-    projected = jnp.dot(owner_att, out_full[:att_all], preferred_element_type=f32) + jnp.dot(
-        gated_norm, out_full[att_all:], preferred_element_type=f32
-    )
+    gated_r = gated_b.astype(f32)
+    gain_b = lax.dynamic_slice_in_dim(gate_gain, branch_id * ssm_cols, ssm_cols, 0)
+    ssm_all = gate_gain.shape[0]
+    squares = branch_sum(jnp.sum(gated_r * gated_r, axis=1))
+    inverse_g = lax.rsqrt(squares / ssm_all + EPSILON)[:, None]
+    scaled_g = gated_r * inverse_g
+    mixed_out = jnp.concatenate([attn_out, (scaled_g * gain_b).astype(bf16)], axis=1)
+    projected = branch_scatter(jnp.dot(mixed_out, w_out_b, preferred_element_type=f32))
     middle = x_rows + projected
     scaled2, inverse2 = rms_parts(middle)
-    normed2 = (scaled2 * norm2_gain).astype(bf16)
-    gate_val = jnp.dot(normed2, gate_full, preferred_element_type=f32)
-    up_val = jnp.dot(normed2, up_full, preferred_element_type=f32)
+    normed2 = branch_gather((scaled2 * norm2_gain).astype(bf16))
+    gate_up = jnp.dot(normed2, w_gu, preferred_element_type=f32)
+    gate_val = gate_up[:, :hidden_b]
+    up_val = gate_up[:, hidden_b:]
     sig_gate = jax.nn.sigmoid(gate_val)
     silu_gate = gate_val * sig_gate
     hidden = (silu_gate * up_val).astype(bf16)
-    y_out = (middle + jnp.dot(hidden, down_full, preferred_element_type=f32)).astype(bf16)
-    grad_down = jnp.dot(hidden.T, d_out, preferred_element_type=f32)
-    grad_hidden = jnp.dot(d_out, down_full.T, preferred_element_type=f32)
+    grad_hidden = lax.dot_general(
+        d_out_g, w_down_b, (((1,), (1,)), ((), ())), preferred_element_type=f32
+    )
     grad_gate = (grad_hidden * up_val * sig_gate * (1.0 + gate_val * (1.0 - sig_gate))).astype(bf16)
     grad_up = (grad_hidden * silu_gate).astype(bf16)
-    grad_w_gate = jnp.dot(normed2.T, grad_gate, preferred_element_type=f32)
-    grad_w_up = jnp.dot(normed2.T, grad_up, preferred_element_type=f32)
-    grad_normed2 = jnp.dot(grad_gate, gate_full.T, preferred_element_type=f32) + jnp.dot(
-        grad_up, up_full.T, preferred_element_type=f32
-    )
+    grad_gu = jnp.concatenate([grad_gate, grad_up], axis=1)
+    grad_normed2 = branch_scatter(
+        lax.dot_general(grad_gu, w_gu, (((1,), (1,)), ((), ())), preferred_element_type=f32)
+    )
+    y_out = (
+        middle + branch_scatter(jnp.dot(hidden, w_down_b, preferred_element_type=f32))
+    ).astype(bf16)
     grad_middle, grad_n2 = rms_backward(grad_normed2, scaled2, inverse2, norm2_gain)
     grad_middle = grad_middle + d_out.astype(f32)
-    grad_proj = grad_middle.astype(bf16)
-    grad_w_out = jnp.concatenate(
+    grad_proj = branch_gather(grad_middle.astype(bf16))
+    grad_mixed = lax.dot_general(
+        grad_proj, w_out_b, (((1,), (1,)), ((), ())), preferred_element_type=f32
+    )
+    back_att = grad_mixed[:, :att_cols].astype(bf16)
+    grad_gnormed = grad_mixed[:, att_cols:]
+    grad_scaled = grad_gnormed * gain_b
+    mean_g = branch_sum(jnp.sum(grad_scaled * scaled_g, axis=1))[:, None] / ssm_all
+    back_ssm = (inverse_g * (grad_scaled - scaled_g * mean_g)).astype(bf16)
+    grad_gate_gain = jnp.sum(grad_gnormed * scaled_g, axis=0)
+
+    def over_rows(left, right):
+        return lax.dot_general(
+            left, right, (((0,), (0,)), ((), ())), preferred_element_type=f32
+        ).astype(bf16)
+
+    def strips(rows_all):
+        wide = rows_all.reshape((groups, parts, strip) + rows_all.shape[1:])
+        return jnp.swapaxes(wide, 0, 1).reshape((parts, groups * strip) + rows_all.shape[1:])
+
+    terms2 = jnp.concatenate(
         [
-            jnp.dot(owner_att.T, grad_proj, preferred_element_type=f32),
-            jnp.dot(gated_norm.T, grad_proj, preferred_element_type=f32),
+            over_rows(mixed_out, grad_proj).reshape(parts, chunk, dim),
+            over_rows(hidden, d_out_g).reshape(parts, chunk, dim),
+            strips(over_rows(normed2, grad_gu)),
         ],
-        axis=0,
-    )
-    grad_att = jnp.dot(grad_proj, out_full[:att_all].T, preferred_element_type=f32).astype(bf16)
-    grad_gnormed = jnp.dot(grad_proj, out_full[att_all:].T, preferred_element_type=f32)
-    grad_ssm_in, grad_gate_gain = rms_backward(grad_gnormed, scaled_g, inverse_g, gate_gain)
-    back_att, back_ssm = (
-        lax.all_to_all(grad_att, "branch", split_axis=1, concat_axis=0, tiled=True),
-        lax.all_to_all(grad_ssm_in.astype(bf16), "branch", split_axis=1, concat_axis=0, tiled=True),
-    )
+        axis=1,
+    )
+    own2 = lax.psum_scatter(terms2, "seq", scatter_dimension=0)
+    own_rows = lax.ppermute(own2[: 2 * chunk], ("branch", "seq"), from_heads).astype(f32)
+    grad_w_out = own_rows[:chunk]
+    grad_w_down = own_rows[chunk:]
+    own_gu = lax.all_to_all(
+        own2[2 * chunk :].reshape(groups, strip, 2 * hidden_b), "branch", 0, 0, tiled=True
+    ).astype(f32)
+
+    def all_columns(blocks):
+        blocks = jnp.swapaxes(blocks, 0, 1)
+        return jnp.concatenate(
+            [blocks[:, :, :hidden_a].reshape(strip, -1), blocks[:, :, hidden_a:].reshape(strip, -1)],
+            axis=1,
+        )
+
+    grad_w_gate = all_columns(own_gu[:, :, :hidden_b])
+    grad_w_up = all_columns(own_gu[:, :, hidden_b:])
     (
         grad_state_in,
         grad_intra,
@@ -487,9 +582,10 @@
             (grad_x_fin + grad_x_span, grad_b, grad_c_fin + grad_c_span, grad_dt, grad_rate)
         )
     )
-    rim_back_x, rim_back_bc = from_behind(
-        (grad_x_ext[:rim_rows], grad_bc_ext[:rim_rows]), "seq", -1
-    )
+    rim_back = from_behind(
+        jnp.concatenate([grad_x_ext[:rim_rows], grad_bc_ext[:rim_rows]], axis=1), "seq", -1
+    )
+    rim_back_x, rim_back_bc = (rim_back[:, :ssm_cols], rim_back[:, ssm_cols:])
     grad_x_pre = grad_x_ext[rim_rows:].at[seq_rows - rim_rows :].add(rim_back_x)
     grad_bc_pre = grad_bc_ext[rim_rows:].at[seq_rows - rim_rows :].add(rim_back_bc)
     grad_att_rows = back_att.reshape(seq_rows, att_heads, HEAD)
@@ -512,8 +608,6 @@
     piece_delta = lax.all_gather(delta_rows.astype(jnp.bfloat16), "seq", axis=0, tiled=True).astype(
         jnp.float32
     )
-    piece_keys = lax.all_gather(keys_rot, "seq", axis=0, tiled=True)
-    piece_values = lax.all_gather(values_b, "seq", axis=0, tiled=True)
     amount = piece_q.shape[0]
     grad_q_now = empty3
     grad_k_now = empty_keys
@@ -551,75 +645,113 @@
     grad_k_raw = rotate(grad_k_now.reshape(seq_rows, 1, HEAD), position, -1.0).reshape(
         seq_rows, HEAD
     )
-    grad_side = jnp.concatenate([grad_k_raw, grad_v_now, grad_bc_pre], axis=1)
-    grad_zx = jnp.concatenate([grad_z, grad_x_pre], axis=1).astype(bf16)
-    grad_dt_b = grad_dt_raw.astype(bf16)
-    grad_group = (
-        jnp.dot(grad_q_raw, mix_full[:, :att_cols].T, preferred_element_type=f32)
-        + jnp.dot(grad_zx, mix_full[:, att_cols:].T, preferred_element_type=f32)
-        + jnp.dot(grad_dt_b, dt_full.T, preferred_element_type=f32)
-        + jnp.dot(grad_side, side_w.astype(f32).T, precision=HIGHEST)
-    )
-    grad_normed1 = lax.psum_scatter(
-        grad_group.astype(jnp.bfloat16), "branch", scatter_dimension=0, tiled=True
-    ).astype(jnp.float32)
-    grad_x1, grad_n1 = rms_backward(grad_normed1, scaled1, inverse1, norm1_gain)
-    grad_x_rows = grad_middle + grad_x1
-    grad_mix = jnp.concatenate(
+    pad_cols = dt_pad - ssm_heads
+    grad_pre = jnp.concatenate(
         [
-            jnp.dot(group_in.T, grad_q_raw, preferred_element_type=f32),
-            jnp.dot(group_in.T, grad_zx, preferred_element_type=f32),
+            grad_q_raw,
+            grad_k_raw.astype(bf16),
+            grad_v_now.astype(bf16),
+            grad_z.astype(bf16),
+            grad_x_pre.astype(bf16),
+            grad_bc_pre.astype(bf16),
+            jnp.pad(grad_dt_raw, ((0, 0), (0, pad_cols))).astype(bf16),
         ],
         axis=1,
     )
-    grad_dt_w = jnp.dot(group_in.T, grad_dt_b, preferred_element_type=f32)
-    grad_side_w = jnp.dot(group_in.astype(f32).T, grad_side, precision=HIGHEST)
-    kv_pick = (jnp.arange(KV) == kv_head).astype(f32)
-    width_rows = grad_side_w.shape[0]
+    grad_group = lax.dot_general(
+        grad_pre, w1, (((1,), (1,)), ((), ())), preferred_element_type=f32
+    )
+    grad_n1 = jnp.sum(grad_group * group_in.astype(f32), axis=0) / norm1_gain
+    grad_w1 = over_rows(group_in, grad_pre)
+    tall = groups * strip
+
+    def to_column(vector, rows_each):
+        padded = jnp.pad(vector.reshape(parts, rows_each), ((0, 0), (0, tall - rows_each)))
+        return padded[:, :, None]
+
+    def to_columns(matrix, rows_each):
+        wide = jnp.swapaxes(matrix.reshape(matrix.shape[0], parts, rows_each), 0, 1)
+        wide = jnp.pad(wide, ((0, 0), (0, 0), (0, tall - rows_each)))
+        return jnp.swapaxes(wide, 1, 2)
+
+    bc_each = conv_bc.shape[1] // (groups * parts)
+    x_each = ssm_cols // parts
+    bc_wide = grad_conv_bc.reshape(CONV, groups, parts, bc_each)
+    bc_wide = jnp.pad(bc_wide, ((0, 0), (0, 0), (0, 0), (0, strip - bc_each)))
+    bc_wide = jnp.transpose(bc_wide, (2, 1, 3, 0)).reshape(parts, tall, CONV)
+    heads3 = jnp.concatenate([grad_a_log, grad_dt_bias, grad_skip])
+    heads3 = jnp.broadcast_to(heads3[None, None, :], (parts, tall, 3 * ssm_heads))
+    small = jnp.concatenate(
+        [
+            strips(jnp.stack([grad_n1, grad_n2], axis=1)),
+            bc_wide,
+            to_column(grad_gate_gain, x_each),
+            to_columns(grad_conv_x, x_each),
+            heads3,
+        ],
+        axis=2,
+    )
+    small = jnp.pad(small, ((0, 0), (0, 0), (0, pad_cols - small.shape[2]))).astype(bf16)
+
+    def plain(rows_all):
+        return rows_all.reshape(parts, tall, rows_all.shape[1])
+
+    terms1 = jnp.concatenate(
+        [
+            plain(grad_w1[:, :at_k]),
+            strips(grad_w1[:, at_k:at_z]),
+            plain(grad_w1[:, at_z:at_bc]),
+            strips(grad_w1[:, at_bc:at_dt]),
+            plain(grad_w1[:, at_dt : at_dt + ssm_heads]),
+            small,
+        ],
+        axis=2,
+    )
+    grad_normed1 = branch_scatter(grad_group)
+    own1 = lax.psum_scatter(terms1, "seq", scatter_dimension=0)
+    at_s = at_dt + ssm_heads
+    own_f = own1.astype(f32)
+    grad_mix = jnp.concatenate([own_f[:, :at_k], own_f[:, at_z:at_bc]], axis=1)
+    grad_dt_w = own_f[:, at_dt:at_s]
+    shared_part = jnp.concatenate(
+        [own1[:, at_k:at_z], own1[:, at_bc:at_dt], own1[:, at_s : at_s + 2 + CONV]], axis=1
+    ).reshape(groups, strip, -1)
+    blocks = lax.all_to_all(shared_part, "branch", 0, 0, tiled=True).astype(f32)
+    per_kv = groups // KV
+    bc_cols = at_dt - at_bc
     grad_shared = jnp.concatenate(
         [
-            (grad_side_w[:, None, :HEAD] * kv_pick[None, :, None]).reshape(width_rows, kv_cols),
-            (grad_side_w[:, None, HEAD : 2 * HEAD] * kv_pick[None, :, None]).reshape(
-                width_rows, kv_cols
-            ),
-            grad_side_w[:, 2 * HEAD :],
-        ],
+            jnp.sum(blocks[h * per_kv : (h + 1) * per_kv, :, at : at + HEAD], axis=0)
+            for at in (0, HEAD)
+            for h in range(KV)
+        ]
+        + [jnp.sum(blocks[:, :, 2 * HEAD : 2 * HEAD + bc_cols], axis=0)],
         axis=1,
     )
-    reduced = (
-        lax.psum_scatter(grad_n1, ("branch", "seq"), scatter_dimension=0, tiled=True),
-        lax.psum_scatter(grad_shared, ("branch", "seq"), scatter_dimension=0, tiled=True),
-        lax.psum_scatter(grad_conv_bc, ("branch", "seq"), scatter_dimension=1, tiled=True),
-        lax.psum_scatter(grad_gate_gain, ("branch", "seq"), scatter_dimension=0, tiled=True),
-        lax.psum_scatter(grad_w_out, ("branch", "seq"), scatter_dimension=0, tiled=True),
-        lax.psum_scatter(grad_n2, ("branch", "seq"), scatter_dimension=0, tiled=True),
-        lax.psum_scatter(grad_w_gate, ("branch", "seq"), scatter_dimension=0, tiled=True),
-        lax.psum_scatter(grad_w_up, ("branch", "seq"), scatter_dimension=0, tiled=True),
-        lax.psum_scatter(grad_down, ("branch", "seq"), scatter_dimension=0, tiled=True),
-    )
-    branch_red = (
-        *side_by_side((grad_mix.astype(jnp.bfloat16), grad_dt_w.astype(jnp.bfloat16)), "seq", 0, 1),
-        sent_and_summed(grad_conv_x.astype(jnp.bfloat16), "seq", 1),
-    )
-    head_red = lax.psum((grad_a_log, grad_dt_bias, grad_skip), "seq")
+    gains = jnp.sum(blocks[:, :, 2 * HEAD + bc_cols :], axis=0)
+    at_g = at_s + 2 + CONV
+    grad_gain_g = own_f[:x_each, at_g]
+    grad_cx = own_f[:x_each, at_g + 1 : at_g + 1 + CONV].T
+    at_h = at_g + 1 + CONV
+    grad_x1, unused_n1 = rms_backward(grad_normed1, scaled1, inverse1, norm1_gain)
     return (
         y_out,
-        grad_x_rows,
-        reduced[0],
-        branch_red[0],
-        branch_red[1],
-        reduced[1],
-        branch_red[2],
-        reduced[2],
-        head_red[0],
-        head_red[1],
-        head_red[2],
-        reduced[3],
-        reduced[4],
-        reduced[5],
-        reduced[6],
-        reduced[7],
-        reduced[8],
+        grad_middle + grad_x1,
+        gains[:, 0],
+        grad_mix,
+        grad_dt_w,
+        grad_shared,
+        grad_cx,
+        gains[:bc_each, 2:].T,
+        own_f[0, at_h : at_h + ssm_heads],
+        own_f[0, at_h + ssm_heads : at_h + 2 * ssm_heads],
+        own_f[0, at_h + 2 * ssm_heads : at_h + 3 * ssm_heads],
+        grad_gain_g,
+        grad_w_out,
+        gains[:, 1],
+        grad_w_gate,
+        grad_w_up,
+        grad_w_down,
     )
 
 

time: 1350 us -> 754 us (0.56)
  waiting for transfers between devices: 655 us -> 86.7 us
  blocking collectives: 217 us -> 127 us
  local copies, waits for them, and re-layouts: 78.7 us -> 152 us
  matrix products: 191 us -> 144 us
  other arithmetic: 140 us -> 161 us
  starting transfers between devices: 34.6 us -> 48.4 us
    reduce_scatter x5 -> x2, waiting for transfers between devices: 608 us -> 25.4 us  [the longest x1 25.4 us: shards(): own2 = lax.psum_scatter(terms2, 'seq', scatter_dimension=0)]
    all_gather x3 -> x0, blocking collectives: 50.4 us -> none  [the longest x1 19.3 us: over_keys(): lax.all_gather(values_b, 'seq', axis=0, tiled=True)]
    all_to_all x0 -> x3, blocking collectives: none -> 47.9 us  [the longest x2 34.7 us: branch_scatter(): lax.all_to_all(blocks, 'branch', 0, 0, tiled=True).astype(f32)]
    unnamed x2 -> x1, blocking collectives: 61.4 us -> 14.9 us
    psum x1 -> x0, blocking collectives: 44.7 us -> none  [shards(): head_red = lax.psum((grad_a_log, grad_dt_bias, grad_skip), 'seq')]
    dot_general x27 -> x12, matrix products: 72.5 us -> 28.4 us  [the longest x4 8.77 us: over_rows(): lax.dot_general(left, right, (((0,), (0,)), ((), ())), preferred_element_...]
    all_to_all x6 -> x7, waiting for transfers between devices: 3.95 us -> 28.9 us  [the longest x2 20 us: branch_scatter(): lax.all_to_all(blocks, 'branch', 0, 0, tiled=True).astype(f32)]
    slice x8 -> x31, local copies, waits for them, and re-layouts: 3.6 us -> 28.1 us  [the longest x1 2.96 us: shards(): w_down_b = w2[:, chunk:2 * chunk].reshape(parts * chunk, dim)]
  transfers between devices with their start and end apart: 25 -> 24, of which waited for: 11 -> 12; matrix products, arithmetic and copies ran while one was open for 26% -> 51% of each run, Pallas kernels for 0% -> 0%
where the time goes in v1:
time: 754 us; the launch traced here: 741 us
  other arithmetic  161 us (21%)
  local copies, waits for them, and re-layouts  152 us (20%)
  matrix products  144 us (19%)
  blocking collectives  127 us (17%)
  waiting for transfers between devices  86.7 us (11%)
  starting transfers between devices  48.4 us (6%)
  between operations  18.8 us (2%)
    all_to_all x2, blocking collectives, branch_scatter(): lax.all_to_all(blocks, 'branch', 0, 0, tiled=True).astype(f32)  34.7 us
    dynamic_update_slice x28, local copies, waits for them, and re-layouts, span_all(): composed, unused = lax.scan(compose, initial, (span_decay, span_state))  25.7 us
    reduce_scatter x1, waiting for transfers between devices, shards(): own2 = lax.psum_scatter(terms2, 'seq', scatter_dimension=0)  25.4 us
    dot_general x3, matrix products, raw_scores(): jnp.einsum('rhd,nd->rhn', queries, piece_keys, preferred_element_type=f32)  23 us
    all_to_all x2, waiting for transfers between devices, branch_scatter(): lax.all_to_all(blocks, 'branch', 0, 0, tiled=True).astype(f32)  20 us
    all_gather x1, waiting for transfers between devices, shards(): w1 = lax.all_gather(w1_part, 'seq', axis=0, tiled=True)  18.4 us
    all_gather x1, blocking collectives, shards(): lax.all_gather(log_total.astype(jnp.bfloat16), 'seq', axis=0, tiled=True)  18.1 us
    unnamed x342, local copies, waits for them, and re-layouts  17.6 us
  transfers between devices with their start and end apart: 24, of which 12 were waited for; matrix products, arithmetic and copies ran while one was open for 51% of the time, Pallas kernels for 0%

profile of v1, /device:TPU:4, one launch (start us, length us, event | category | flops | bytes accessed | tf_op | source)
XLA Modules:
  0.0 740.6 jit_solution(5703898402947534241)
XLA Ops:
  34.3 18.4 %all-gather.10.cloned.1.call-done = bf16[1024,1408]{1,0:T(8,128)(2,1)} async-done(((bf16[128,1408]{1,0:T(8,128)(2,1)}), bf16[1024,1408]{1,0:T(8,128)(2,1)}) %all-gather.10.cloned.1.call-update) | async-done | bytes 2883600 | tf_op jit(solution)/shard_map/all_gather | solution.py:329
  113.3 21.7 %while.106 = (s32[]{:T(128)}, f32[6]{0:T(128)}, f32[6,64,128]{2,1,0:T(8,128)S(1)}, f32[4,6]{1,0:T(4,128)}, f32[4,6,64,128]{3,2,1,0:T(8,128)}, /*index=5*/f32[4,6...) while((s32[]{:T(128)}, f32[6]{0:T(128)}, ...), condition=%wide.region_17.18_spmd.clone, body=%wide.region_16.17_spmd.clone.sunk | while | flops 196623 | bytes 985405 | solution.py:209
  135.0 16.4 %all-gather.1 = bf16[48,64,128]{2,1,0:T(8,128)(2,1)} all-gather(bf16[6,64,128]{2,1,0:T(8,128)(2,1)S(1)} %convert_element_type.328), channel_id=3, replica_groups=mesh['branch'=4,'seq'=8] {'seq'}, dimensions={0}, use_global_device_ids=true | all-gather | bytes 884736 | tf_op jit(solution)/shard_map/all_gather | solution.py:28
  152.3 14.9 %all-reduce.26 = bf16[48]{0:T(256)(128)(2,1)S(1)} all-reduce(bf16[48]{0:T(256)(128)(2,1)S(1)} %dynamic-update-slice.6), channel_id=2, replica_groups=mesh['branch'=4,'seq'=8] {'seq'}, use_global_device_ids=true, to_apply=%add.26 | all-reduce | flops 48 | bytes 192
  180.0 14.4 %while.104 = (s32[]{:T(128)}, f32[6,64,128]{2,1,0:T(8,128)S(1)}, f32[4,6,64,128]{3,2,1,0:T(8,128)}, f32[4,6,1,1]{1,3,2,0:T(1,128)}, f32[4,6]{1,0:T(4,128)}, /*index=5*/f32[4,6,64,128]{3,2,1,0:T(8,128)}, s32[]{:T(128)}) while((s32[]{:T(128)}, f32[6,64,128]{2,1,0:T(8,128)S(1)}, f32[4,6,64,128]{3,2,1,0:T(8,128)}, f32[4,6,1,1]{1,3,2,0:T(1,128)}, ...), condition=%wide.region_21.22_spmd, body=%wide.region_20.21_spmd.sunk | while | flops 98306 | bytes 985245 | solution.py:222
  218.8 15.0 %conditional.4 = (f32[512,2]{0,1:T(2,128)}, f32[512,2]{0,1:T(2,128)S(1)}) conditional(s32[]{:T(128)} %convert_element_type.317, () %tuple.162, (s32[512]{0:T(512)}, s32[5]{0:T(128)}, s32[512]{0:T(512)}, bf16[512,2,64]{0,2,1:T(8,128)(2,1)S(1)}, bf16[4096,64]{0,1:T(8,128)(2,1)}) %tuple.418), branch_computations={%region_4.5_spmd, %region_5.10_spmd} | conditional | flops 576773120 | bytes 40566864 | solution.py:421
  235.1 29.7 %conditional.5 = (f32[512,2,64]{0,2,1:T(8,128)S(1)}, f32[512,2,64]{0,2,1:T(8,128)S(1)}, bf16[512,128]{1,0:T(8,128)(2,1)S(1)}) conditional(s32[]{:T(128)} %convert_element_type.317, () %tuple.161, (s32[512]{0:T(512)}, s32[5]{0:T(128)}, s32[512]{0:T(512)}, bf16[512,2,64]{0,2,1:T(8,128)(2,1)S(1)}, bf16[4096,64]{0,1:T(8,128)(2,1)}, ...), branch_computations={%region_10.11_spmd, %region_11.14_spmd} | conditional | flops 1663164416 | bytes 67711288 | solution.py:446
  268.7 15.2 %all_to_all.50 = bf16[4,128,1024]{2,1,0:T(8,128)(2,1)S(1)} all-to-all(bf16[4,128,1024]{2,1,0:T(8,128)(2,1)S(1)} %bitcast.436), channel_id=1, replica_groups=mesh['branch'=4,'seq'=8] {'branch'}, dimensions={0} | all-to-all | bytes 2097152 | tf_op jit(solution)/shard_map/all_to_all | solution.py:314
  284.5 13.3 %all_to_all.51 = bf16[4,128,1024]{2,1,0:T(8,128)(2,1)} all-to-all(bf16[4,128,1024]{2,1,0:T(8,128)(2,1)S(1)} %broadcast_in_dim.319), channel_id=1, replica_groups=mesh['branch'=4,'seq'=8] {'branch'}, dimensions={0} | all-to-all | bytes 2097152 | tf_op jit(solution)/shard_map/all_to_all | solution.py:308
  348.3 18.1 %all_gather.53 = bf16[4096,2]{0,1:T(2,128)(2,1)S(1)} all-gather(bf16[512,2]{0,1:T(2,128)(2,1)S(1)} %copy-done.141), channel_id=1, replica_groups=mesh['branch'=4,'seq'=8] {'seq'}, dimensions={0}, use_global_device_ids=true | all-gather | bytes 18432 | tf_op jit(solution)/shard_map/all_gather | solution.py:605
  376.9 12.7 %all_gather.55 = bf16[4096,2]{0,1:T(2,128)(2,1)S(1)} all-gather(bf16[512,2]{0,1:T(2,128)(2,1)S(1)} %convert_element_type.350), channel_id=1, replica_groups=mesh['branch'=4,'seq'=8] {'seq'}, dimensions={0}, use_global_device_ids=true | all-gather | bytes 18432 | tf_op jit(solution)/shard_map/all_gather | solution.py:608
  390.3 30.4 %conditional.6 = (f32[512,2,32]{0,2,1:T(8,128)S(1)}, f32[512,2,32]{0,2,1:T(8,128)S(1)}) conditional(s32[]{:T(128)} %convert_element_type.317, () %tuple.168, (s32[512]{0:T(512)}, s32[5]{0:T(128)}, s32[512]{0:T(512)}, bf16[512,2,64]{0,2,1:T(8,128)(2,1)S(1)}, bf16[4096,64]{0,1:T(8,128)(2,1)}, /*index=5*/f32[512,2]{0,1:T(2,128)}, ...), branch_computations={%region_29.30_spmd, %region_30.33_spmd} | conditional | flops 1642192896 | bytes 40939628 | solution.py:641
  404.6 14.9 %fusion.24 = f32[512,2,64]{0,2,1:T(8,128)} fusion(f32[512,2,4096]{2,0,1:T(8,128)} %fusion.28, bf16[512,2,64]{0,2,1:T(8,128)(2,1)S(1)} %copy-done.51, f32[512,2]{0,1:T(2,128)} %get-tuple-element.731, f32[512,2]{0,1:T(2,128)} %get-tuple-element.728, pred[512,4096]{1,0:T(8,128)(4,1)} %fusion.22, bf16[4096,64]{0,1:T(8,128)(2,1)} %get-tuple-element.730, ...), kind=kOutput, calls=%fused_computation.40 | convolution fusion | flops 1098973184 | bytes 20324352 | tf_op jit(solution)/shard_map/cond/branch_1_fun/rhn,nd->rhd/dot_general | solution.py:618
  443.0 15.1 %while.108 = (s32[]{:T(128)}, f32[6,64,128]{2,1,0:T(8,128)S(1)}, f32[4,6]{1,0:T(4,128)}, f32[4,6,64,128]{3,2,1,0:T(8,128)}, f32[4,6,64,128]{3,2,1,0:T(8,128)}, /...) while((s32[]{:T(128)}, f32[6,64,128]{2,1,0:T(8,128)S(1)}, ...), condition=%wide.region_41.42_spmd.clone, body=%wide.region_39.41_spmd.clone.sunk | while | flops 294910 | bytes 1179932 | solution.py:222
  458.0 17.0 %all-gather.3 = bf16[48,64,128]{2,1,0:T(8,128)(2,1)} all-gather(bf16[6,64,128]{2,1,0:T(8,128)(2,1)S(1)} %convert_element_type.356), channel_id=5, replica_groups=mesh['branch'=4,'seq'=8] {'seq'}, dimensions={0}, use_global_device_ids=true | all-gather | bytes 884736 | tf_op jit(solution)/shard_map/all_gather | solution.py:51
  475.0 14.0 %while.109 = (s32[]{:T(128)}, f32[6,64,128]{2,1,0:T(8,128)S(1)}, s32[]{:T(128)}, bf16[8,6,64,128]{3,2,1,0:T(8,128)(2,1)}, bf16[8,6]{1,0:T(8,128)(2,1)}, /*index=5*/s32[]{:T(128)}, s32[]{:T(128)}, s32[]{:T(128)}, s32[]{:T(128)}) while((s32[]{:T(128)}, f32[6,64,128]{2,1,0:T(8,128)S(1)}, s32[]{:T(128)}, ...), condition=%wide.region_43.44_spmd.clone, body=%wide.region_42.43_spmd.clone.sunk | while | flops 245774 | bytes 491747 | solution.py:69
  490.1 12.4 %while.105 = (s32[]{:T(128)}, f32[6]{0:T(128)S(1)}, f32[6,64,128]{2,1,0:T(8,128)S(1)}, f32[4,6]{1,0:T(4,128)S(1)}, f32[4,6,64,128]{3,2,1,0:T(8,128)}, /*index=5*...) while((s32[]{:T(128)}, f32[6]{0:T(128)S(1)}, ...), condition=%wide.region_47.48_spmd, body=%wide.region_45.47_spmd.sunk | while | flops 147471 | bytes 983477 | solution.py:209
  564.0 34.0 %conditional.7 = (f32[512,1,32]{0,2,1:T(8,128)S(1)}, f32[512,1,32]{0,2,1:T(8,128)S(1)}, bf16[512,64]{1,0:T(8,128)(2,1)S(1)}) conditional(s32[]{:T(128)} %convert_element_type.347, () %tuple.170, (s32[512]{0:T(512)S(1)}, s32[512]{0:T(512)S(1)}, s32[5]{0:T(128)S(1)}, bf16[4096,2,64]{0,2,1:T(8,128)(2,1)}, bf16[512,64]{0,1:T(8,128)(2,1)S(1)}, ...), branch_computations={%region_34.35_spmd, %region_35.38_spmd} | conditional | flops 2195841024 | bytes 61935760 | solution.py:643
  564.0 9.4 %fusion.49 = f32[4096,2,512]{2,0,1:T(8,128)} fusion(bf16[4096,2,64]{0,2,1:T(8,128)(2,1)} %get-tuple-element.735, bf16[512,64]{0,1:T(8,128)(2,1)S(1)} %get-tuple-element.736), kind=kOutput, calls=%fused_computation.65 | convolution fusion | flops 536870912 | bytes 17891328 | tf_op jit(solution)/shard_map/cond/branch_1_fun/nhd,rd->nhr/dot_general | solution.py:628
  576.0 13.3 %fusion.43 = f32[512,1,64]{0,2,1:T(8,128)S(1)} fusion(bf16[4096,2,64]{0,2,1:T(8,128)(2,1)} %get-tuple-element.735, f32[4096,2,512]{2,0,1:T(8,128)} %fusion.49, bf16[4096,2,64]{0,2,1:T(8,128)(2,1)} %get-tuple-element.738, f32[4096,2]{0,1:T(2,128)S(1)} %copy-done.112, f32[4096,2]{0,1:T(2,128)S(1)} %copy-done.111, pred[4096,512]{1,0:T(8,128)(4,1)S(1)} %fusion.35, ...), kind=kOutput, calls=%fused_computation.60 | convolution fusion | flops 1098940416 | bytes 21233664 | tf_op jit(solution)/shard_map/cond/branch_1_fun/nhr,nhd->rd/dot_general | solution.py:633
  631.0 19.5 %all_to_all.52 = bf16[4,128,1024]{2,1,0:T(8,128)(2,1)} all-to-all(bf16[4,128,1024]{2,1,0:T(8,128)(2,1)S(1)} %bitcast.435), channel_id=1, replica_groups=mesh['branch'=4,'seq'=8] {'branch'}, dimensions={0} | all-to-all | bytes 2097152 | tf_op jit(solution)/shard_map/all_to_all | solution.py:314
  657.2 11.5 %all-to-all-done.7 = bf16[4,128,1024]{2,1,0:T(8,128)(2,1)S(1)} async-done(((bf16[4,128,1024]{2,1,0:T(8,128)(2,1)}), bf16[4,128,1024]{2,1,0:T(8,128)(2,1)S(1)}, u32[]{:S(2)}, u32[]{:S(2)}) %all-to-all-start.7) | async-done | bytes 1048608 | tf_op jit(solution)/shard_map/all_to_all | solution.py:314
  684.2 25.4 %reduce-scatter.5.cloned.1.call-done = bf16[1,256,1024]{2,1,0:T(8,128)(2,1)} async-done(((bf16[8,256,1024]{2,1,0:T(8,128)(2,1)}), bf16[1,256,1024]{2,1,0:T(8,128)(2,1)}) %reduce-scatter.5.cloned.1.call-update) | async-done | bytes 524304 | tf_op jit(solution)/shard_map/reduce_scatter | solution.py:546
  721.8 10.8 %collective-permute-done.9 = bf16[128,1024]{1,0:T(8,128)(2,1)S(1)} collective-permute-done((bf16[128,1024]{1,0:T(8,128)(2,1)S(1)}, bf16[128,1024]{1,0:T(8,128)(2,1)S(1)}, u32[]{:S(2)}, u32[]{:S(2)}) %collective-permute-start.9) | collective-permute-done | bytes 262176 | tf_op jit(solution)/shard_map/ppermute | solution.py:547
  (799 shorter events, 497.3 us)
Async XLA Ops:
  7.2 45.5 %all-gather.10.cloned.1.call-start = ((), (), s32[]{:S(2)}) async-start(), calls=%async_computation.12 | async-start | bytes 3244032 | tf_op jit(solution)/shard_map/all_gather | solution.py:329
  15.7 18.6 %all-to-all-start = ((bf16[4,128,1024]{2,1,0:T(8,128)(2,1)}), bf16[4,128,1024]{2,1,0:T(8,128)(2,1)S(1)}, u32[]{:S(2)}, u32[]{:S(2)}) async-start(bf16[4,128,1024]{2,1,0:T(8,128)(2,1)} %broadcast_in_dim.314), calls=%async_computation | async-start | bytes 2097152 | tf_op jit(solution)/shard_map/all_to_all | solution.py:308
  19.9 196.6 %all-gather.12.cloned.1.call-start = ((), (), s32[]{:S(2)}) async-start(), calls=%async_computation.13 | async-start | bytes 1179648 | tf_op jit(solution)/shard_map/all_gather | solution.py:394
  21.6 52.2 %collective-permute-start.4 = (bf16[128,1024]{1,0:T(8,128)(2,1)}, bf16[128,1024]{1,0:T(8,128)(2,1)}, u32[]{:S(2)}, u32[]{:S(2)}) collective-permute-start(bf16[128,1024]{1,0:T(8,128)(2,1)} %pad_maximum_fusion.10), channel_id=1, source_target_pairs={{0,0},{8,1},{16,8},{24,9},{1,16},{9,17},{17,24},{25,25},{2,2},{10,... | collective-permute-start | bytes 786440 | tf_op jit(solution)/shard_map/ppermute | solution.py:344
  58.6 206.3 %all-gather.18.cloned.1.call-start = ((), (), s32[]{:S(2)}) async-start(), calls=%async_computation.18 | async-start | bytes 4718592 | tf_op jit(solution)/shard_map/all_gather | solution.py:348
  80.5 15.7 %collective-permute-start = (f32[3,640]{1,0:T(4,128)}, f32[3,640]{1,0:T(4,128)}, u32[]{:S(2)}, u32[]{:S(2)}) collective-permute-start(f32[3,640]{1,0:T(4,128)} %slice.475), channel_id=1, source_target_pairs={{0,1},{1,2},{2,3},{3,4},{4,5},{5,6},{6,7},{8,9},{9,10},{10,11},{11... | collective-permute-start | bytes 23048 | tf_op jit(solution)/shard_map/ppermute | solution.py:22
  208.3 4.8 collective-permute-start.1
  209.8 3.9 collective-permute-start.2
  210.4 3.9 collective-permute-start.3
  298.9 14.7 %all-to-all-start.4 = ((bf16[4,128,1024]{2,1,0:T(8,128)(2,1)}), bf16[4,128,1024]{2,1,0:T(8,128)(2,1)}, u32[]{:S(2)}, u32[]{:S(2)}) async-start(bf16[4,128,1024]{2,1,0:T(8,128)(2,1)} %broadcast_in_dim.320), calls=%async_computation.4 | async-start | bytes 2097152 | tf_op jit(solution)/shard_map/all_to_all | solution.py:308
  320.2 13.9 %all-to-all-start.5 = ((bf16[4,128,1024]{2,1,0:T(8,128)(2,1)}), bf16[4,128,1024]{2,1,0:T(8,128)(2,1)}, u32[]{:S(2)}, u32[]{:S(2)}) async-start(bf16[4,128,1024]{2,1,0:T(8,128)(2,1)} %bitcast.434), calls=%async_computation.5 | async-start | bytes 2097152 | tf_op jit(solution)/shard_map/all_to_all | solution.py:314
  325.1 238.8 %all-gather.14.cloned.1.call-start = ((), (), s32[]{:S(2)}) async-start(), calls=%async_computation.14 | async-start | bytes 1179648 | tf_op jit(solution)/shard_map/all_gather | solution.py:603
  338.1 29.5 %all-to-all-start.6 = ((bf16[4,128,1024]{2,1,0:T(8,128)(2,1)}), bf16[4,128,1024]{2,1,0:T(8,128)(2,1)}, u32[]{:S(2)}, u32[]{:S(2)}) async-start(bf16[4,128,1024]{2,1,0:T(8,128)(2,1)} %broadcast_in_dim.321), calls=%async_computation.6 | async-start | bytes 2097152 | tf_op jit(solution)/shard_map/all_to_all | solution.py:308
  343.0 220.8 %all-gather.16.cloned.1.call-start = ((), (), s32[]{:S(2)}) async-start(), calls=%async_computation.15 | async-start | bytes 1179648 | tf_op jit(solution)/shard_map/all_gather | solution.py:604
  371.0 52.8 %collective-permute-start.5 = (f32[512]{0:T(512)}, f32[512]{0:T(512)}, u32[]{:S(2)}, u32[]{:S(2)}) collective-permute-start(f32[512]{0:T(512)} %get-tuple-element.1228), channel_id=1, source_target_pairs={{0,8},{8,16},{16,24},{24,0},{1,9},{9,17},{17,25},{25,1},{2,10},{10... | collective-permute-start | bytes 6152 | tf_op jit(solution)/shard_map/ppermute | solution.py:303
  372.4 51.3 %collective-permute-start.6 = (f32[512]{0:T(512)}, f32[512]{0:T(512)}, u32[]{:S(2)}, u32[]{:S(2)}) collective-permute-start(f32[512]{0:T(512)} %get-tuple-element.1228), channel_id=1, source_target_pairs={{0,16},{8,24},{16,0},{24,8},{1,17},{9,25},{17,1},{25,9},{2,18},{10... | collective-permute-start | bytes 6152 | tf_op jit(solution)/shard_map/ppermute | solution.py:303
  373.0 50.8 %collective-permute-start.7 = (f32[512]{0:T(512)}, f32[512]{0:T(512)}, u32[]{:S(2)}, u32[]{:S(2)}) collective-permute-start(f32[512]{0:T(512)} %get-tuple-element.1228), channel_id=1, source_target_pairs={{0,24},{8,0},{16,8},{24,16},{1,25},{9,1},{17,9},{25,17},{2,26},{10... | collective-permute-start | bytes 6152 | tf_op jit(solution)/shard_map/ppermute | solution.py:303
  390.3 281.1 %reduce-scatter.3.cloned.1.call-start = ((), (), s32[]{:S(2)}) async-start(), calls=%async_computation.16 | async-start | bytes 3244032 | tf_op jit(solution)/shard_map/reduce_scatter | solution.py:711
  543.0 18.9 %collective-permute-start.8 = (f32[3,640]{1,0:T(4,128)}, f32[3,640]{1,0:T(4,128)}, u32[]{:S(2)}, u32[]{:S(2)}) collective-permute-start(f32[3,640]{1,0:T(4,128)} %pad_maximum_fusion.17), channel_id=1, source_target_pairs={{1,0},{2,1},{3,2},{4,3},{5,4},{6,5},{7,6},{9,8},{10,9},{11,10},{12... | collective-permute-start | bytes 23048 | tf_op jit(solution)/shard_map/ppermute | solution.py:22
  619.0 90.5 %reduce-scatter.5.cloned.1.call-start = ((), (), s32[]{:S(2)}) async-start(), calls=%async_computation.17 | async-start | bytes 4718592 | tf_op jit(solution)/shard_map/reduce_scatter | solution.py:546
  650.5 18.2 %all-to-all-start.7 = ((bf16[4,128,1024]{2,1,0:T(8,128)(2,1)}), bf16[4,128,1024]{2,1,0:T(8,128)(2,1)S(1)}, u32[]{:S(2)}, u32[]{:S(2)}) async-start(bf16[4,128,1024]{2,1,0:T(8,128)(2,1)} %bitcast.433), calls=%async_computation.7 | async-start | bytes 2097152 | tf_op jit(solution)/shard_map/all_to_all | solution.py:314
  675.6 7.8 %all-to-all-start.8 = ((bf16[4,32,390]{2,1,0:T(8,128)(2,1)}), bf16[4,32,390]{2,1,0:T(8,128)(2,1)S(1)}, u32[]{:S(2)}, u32[]{:S(2)}) async-start(bf16[4,32,390]{2,1,0:T(8,128)(2,1)} %bitcast.111), calls=%async_computation.9 | async-start | bytes 262144 | tf_op jit(solution)/shard_map/all_to_all | solution.py:719
  711.3 8.8 %all-to-all-start.9 = ((bf16[4,32,1024]{2,1,0:T(8,128)(2,1)}), bf16[4,32,1024]{2,1,0:T(8,128)(2,1)S(1)}, u32[]{:S(2)}, u32[]{:S(2)}) async-start(bf16[4,32,1024]{2,1,0:T(8,128)(2,1)} %bitcast.123), calls=%async_computation.11 | async-start | bytes 524288 | tf_op jit(solution)/shard_map/all_to_all | solution.py:550
  717.0 15.6 %collective-permute-start.9 = (bf16[128,1024]{1,0:T(8,128)(2,1)S(1)}, bf16[128,1024]{1,0:T(8,128)(2,1)S(1)}, u32[]{:S(2)}, u32[]{:S(2)}) collective-permute-start(bf16[128,1024]{1,0:T(8,128)(2,1)S(1)} %get-tuple-element.1391), channel_id=1, source_target_pairs={{0,0},{1,1},{8,2},{9,3},{16,4},{17,5},{24,6},{25,7},{2,8},{3,9},{4... | collective-permute-start | bytes 786440 | tf_op jit(solution)/shard_map/ppermute | solution.py:547
  (171 other events, 1664.4 us)
Sparse Core Ops, SparseCore 0:
  12.5 40.1 all-gather.9
  58.8 20.9 all-gather.11
  81.4 46.7 all-gather.17
  327.2 25.2 all-gather.13
  390.4 20.4 all-gather.15
  619.2 38.5 reduce-scatter.2
  660.1 49.4 reduce-scatter.4
